TPU v7x, 32 devices: a whole 2x2x4 slice. The times are simulated.
32 devices in a mesh: sec: 4 (over y, x), strip: 8 (over z, core).
Axes of the slice: x: 2, y: 2, z: 4, core: 2. Of those that a mesh axis runs over, the one named last changes fastest.
Arguments:
- image: bfloat16 [4, 16, 160, 160], P('sec', 'strip'), may hold values from -6 to 6
- peaks: int32 [4, 16, 2], P('sec', 'strip'), may hold values from 0 to 159
- row_source: int32 [4, 16, 160], P('sec', 'strip'), may hold values from 0 to 159
- row_weight: float32 [4, 16, 160], P('sec', 'strip'), may hold values from 0 to 1
- col_source: int32 [4, 16, 160], P('sec', 'strip'), may hold values from 0 to 159
- col_weight: float32 [4, 16, 160], P('sec', 'strip'), may hold values from 0 to 1
- owner: int32 [4, 2560, 1], P('sec', 'strip'), may hold values from 0 to 7; in each aligned block of 320 rows (0 to 319, 320 to 639, ..., all dimensions but the last counted through in order) at most 160 rows name the same one
- render_row: int32 [4, 2560], P('sec', 'strip'), may hold values from 0 to 319
Outputs:
- render: bfloat16 [4, 2560, 160], P('sec', 'strip')
- corr_map: float32 [4, 16, 160, 160], P('sec', 'strip')
Inputs may be any that keep to these rules, and one draw needn't show every extreme that they name: Among the 320 tile rows of one strip, at most 160 have any one owner; in every draw some strip sends exactly 160 to some owner.
All inputs are finite; a program needn't handle non-finite values.
Results may differ from a plain program's by a relative error of at most 0.012.
Values may be sent and summed in bfloat16 or wider, within the bound.
No kernel may reach another device: no remote copies, remote signals or barrier semaphores. Data moves between devices by JAX's collectives and lax.ppermute only.
A program may use at most 64 MiB of HBM per device.

v0:
```python
import functools

import jax
import jax.numpy as jnp
import numpy as np
from jax import lax
from jax.experimental import pallas as pl
from jax.experimental.pallas import tpu as pltpu
from jax.sharding import PartitionSpec as P

GC = 2
LANES = 128
TWO_PI = 2.0 * 3.141592653589793
F32 = jnp.float32
BF16 = jnp.bfloat16
VMEM_BYTES = 40 * 1024 * 1024


def product(left, right):
    return jnp.dot(left, right, preferred_element_type=F32)


def dft_tables(edge):
    positions = np.arange(edge, dtype=np.int32)
    phases = positions[:, None] * positions[None, :] % edge
    angles = phases.astype(np.float32) * np.float32(TWO_PI / edge)
    return jnp.asarray(np.cos(angles), BF16), jnp.asarray(np.sin(angles), BF16)


def round_up(size, unit):
    return -(-size // unit) * unit


def message_rows(rows):
    return rows + rows // 4 + 16


def call(kernel, out_shape, n_in, smem=(), scratch=(), flops=1000000):
    specs = [
        pl.BlockSpec(memory_space=pltpu.SMEM if i in smem else pltpu.VMEM) for i in range(n_in)
    ]
    outs = jax.tree.map(lambda _: pl.BlockSpec(memory_space=pltpu.VMEM), out_shape)
    return pl.pallas_call(
        kernel,
        out_shape=out_shape,
        in_specs=specs,
        out_specs=outs,
        scratch_shapes=list(scratch),
        compiler_params=pltpu.CompilerParams(vmem_limit_bytes=VMEM_BYTES),
        cost_estimate=pl.CostEstimate(flops=flops, bytes_accessed=500000, transcendentals=0),
    )


def warp_matrix_t(source, weight, edge):
    spots = lax.broadcasted_iota(jnp.int32, (edge, edge), 0)
    following = jnp.where(source == edge - 1, 0, source + 1)
    first = jnp.where(spots == source, weight, 0.0)
    second = jnp.where(spots == following, 1.0 - weight, 0.0)
    return (first + second).astype(BF16)


def base_kernel(
    image_ref, row_src, row_wt, col_src, col_wt, owner_ref, target_ref, out_ref, keys
):
    count, edge, _ = image_ref.shape
    rows = count * edge
    part = rows // 4
    rest = edge - LANES
    pieces = []
    for p in range(count):
        row_t = warp_matrix_t(row_src[p : p + 1, :], row_wt[p : p + 1, :], edge)
        col_t = warp_matrix_t(col_src[p : p + 1, :], col_wt[p : p + 1, :], edge)
        row_warped = lax.dot_general(
            row_t, image_ref[p], (((0,), (0,)), ((), ())), preferred_element_type=F32
        ).astype(BF16)
        base = product(row_warped, col_t)
        out_ref[p * edge : (p + 1) * edge, :] = base[:, :LANES].astype(BF16)
        right = base[:, LANES:]
        pieces += [right[:part], right[part:]]
    out_ref[rows : rows + part, :] = jnp.concatenate(pieces, axis=1).astype(BF16)
    key = owner_ref[...] * rows + target_ref[...]
    keys[...] = jnp.full(keys.shape, -1.0, F32)
    keys[0:1, 0:rows] = (key >> 8).astype(F32)
    keys[8:9, 0:rows] = (key & 255).astype(F32)
    wide = keys.shape[1] // LANES
    blank = jnp.full((8 - wide, LANES), -1.0, F32)
    lines = []
    for half in (0, 8):
        lines += [keys[half : half + 1, j * LANES : (j + 1) * LANES] for j in range(wide)]
        lines += [blank]
    out_ref[rows + part :, :] = jnp.concatenate(lines, axis=0).astype(BF16)


def spectrum_of(pixels, dft_cos, dft_sin, count, edge):
    half_re = product(pixels, dft_cos).astype(BF16)
    half_im = (-product(pixels, dft_sin)).astype(BF16)
    spectra = []
    for p in range(count):
        h_re = half_re[p * edge : (p + 1) * edge]
        h_im = half_im[p * edge : (p + 1) * edge]
        spectra.append(
            (
                product(dft_cos, h_re) + product(dft_sin, h_im),
                product(dft_cos, h_im) - product(dft_sin, h_re),
            )
        )
    return spectra


def spectrum_kernel(image_ref, cos_ref, sin_ref, re_ref, im_ref):
    count, edge, _ = image_ref.shape
    pixels = image_ref[...].reshape(count * edge, edge)
    spectra = spectrum_of(pixels, cos_ref[...], sin_ref[...], count, edge)
    for p, (s_re, s_im) in enumerate(spectra):
        re_ref[p] = s_re
        im_ref[p] = s_im


def surface_kernel(
    message_ref, im_re_ref, im_im_ref, cos_ref, sin_ref, peaks_ref, corr_ref, near_ref, wrapped
):
    count, edge, _ = im_re_ref.shape
    rows = count * edge
    part = rows // 4
    rest = edge - LANES
    dft_cos, dft_sin = cos_ref[...], sin_ref[...]
    side = message_ref[rows : rows + part, :].astype(F32)
    groups = []
    for g in range(4):
        left = message_ref[g * part : (g + 1) * part, :].astype(F32)
        groups.append(jnp.concatenate([left, side[:, g * rest : (g + 1) * rest]], axis=1))
    pixels = jnp.concatenate(groups, axis=0)
    pixels = jnp.where(lax.axis_index("sec") > 0, pixels, 0.0).astype(BF16)
    spectra = spectrum_of(pixels, dft_cos, dft_sin, count, edge)
    lane = lax.broadcasted_iota(jnp.int32, (1, edge), 1)
    out_lane = lax.broadcasted_iota(jnp.int32, (8, LANES), 1)
    near = jnp.zeros((8, LANES), F32)
    for p, (ref_re, ref_im) in enumerate(spectra):
        img_re, img_im = im_re_ref[p], im_im_ref[p]
        cross_re = (ref_re * img_re + ref_im * img_im).astype(BF16)
        cross_im = (ref_im * img_re - ref_re * img_im).astype(BF16)
        back_re = (product(cross_re, dft_cos) - product(cross_im, dft_sin)).astype(BF16)
        back_im = (product(cross_re, dft_sin) + product(cross_im, dft_cos)).astype(BF16)
        corr = (product(dft_cos, back_re) - product(dft_sin, back_im)) * (1.0 / (edge * edge))
        corr_ref[p] = corr
        wrapped[p, 0:edge, :] = corr
        wrapped[p, edge : edge + 8, :] = corr[0:8]
        top = peaks_ref[p, 0] + (edge - 2)
        top = jnp.where(top >= edge, top - edge, top)
        eighth = pl.multiple_of((top >> 3) * 8, 8)
        tile = pltpu.roll(wrapped[p, pl.ds(eighth, 16), :], 16 - (top & 7), 0)[0:8]
        for j in range(5):
            spot = peaks_ref[p, 1] + (j - 2)
            spot = jnp.where(spot < 0, spot + edge, jnp.where(spot >= edge, spot - edge, spot))
            column = jnp.sum(jnp.where(lane == spot, tile, 0.0), axis=1, keepdims=True)
            near = jnp.where(out_lane == 8 * p + j, column, near)
    near_ref[...] = near


def chain_kernel(count, steps, *refs):
    near_refs, (smooth_ref, prior_ref) = refs[:steps], refs[steps:]
    section = lax.axis_index("sec")
    strip = lax.axis_index("strip")
    row = lax.broadcasted_iota(jnp.int32, (8, LANES), 0)
    lane = lax.broadcasted_iota(jnp.int32, (8, LANES), 1)

    def spread(values):
        tile = jnp.broadcast_to(values[0], (8, LANES))
        for p in range(1, count):
            tile = jnp.where(lane >= 8 * p, values[p], tile)
        return tile

    zeros = [jnp.zeros((1, 1), F32)] * count
    smooth_y, smooth_x = zeros, zeros
    for back in range(steps - 1, -1, -1):
        prior_y, prior_x = smooth_y, smooth_x
        near = near_refs[back][...]
        grad_y = 0.5 * (pltpu.roll(near, 7, 0) - pltpu.roll(near, 1, 0))
        grad_x = 0.5 * (pltpu.roll(near, LANES - 1, 1) - pltpu.roll(near, 1, 1))
        corr = near + spread(prior_y) * grad_y + spread(prior_x) * grad_x
        size = jnp.abs(corr)
        below, above = pltpu.roll(corr, 7, 0), pltpu.roll(corr, 1, 0)
        right, left = pltpu.roll(corr, LANES - 1, 1), pltpu.roll(corr, 1, 1)
        flow_y = (below - above) / (jnp.abs(below) + size + jnp.abs(above) + 1.0)
        flow_x = (right - left) / (jnp.abs(right) + size + jnp.abs(left) + 1.0)

        def picked(flow):
            values = []
            for p in range(count):
                here = jnp.logical_and(row == 2, lane == 8 * p + 2)
                spot = jnp.where(here, flow, 0.0)
                values.append(jnp.sum(jnp.sum(spot, axis=1, keepdims=True), axis=0, keepdims=True))
            smooth = []
            for p in range(count):
                total = 0.5 * values[p]
                if p % GC > 0:
                    total = total + 0.25 * values[p - 1]
                if p % GC < GC - 1:
                    total = total + 0.25 * values[p + 1]
                smooth.append(jnp.where(section - back > 0, total, 0.0))
            return smooth

        smooth_y, smooth_x = picked(flow_y), picked(flow_x)

    def laid(values_y, values_x, shape, first):
        out_row = lax.broadcasted_iota(jnp.int32, shape, 0)
        out_lane = lax.broadcasted_iota(jnp.int32, shape, 1)
        tile = jnp.zeros(shape, F32)
        for p in range(count):
            pair = jnp.where(out_row == 0, values_y[p], values_x[p])
            here = jnp.logical_and(out_lane == first + p, out_row < 2)
            tile = jnp.where(here, pair, tile)
        return tile

    smooth_ref[...] = laid(smooth_y, smooth_x, smooth_ref.shape, strip * count)
    prior_ref[...] = laid(prior_y, prior_x, prior_ref.shape, 0)


def map_kernel(corr_ref, prior_ref, out_ref):
    count, edge, _ = corr_ref.shape
    for p in range(count):
        corr = corr_ref[p]
        smooth_y = prior_ref[0:1, p : p + 1]
        smooth_x = prior_ref[1:2, p : p + 1]
        grad_y = jnp.roll(corr, -1, axis=0) - jnp.roll(corr, 1, axis=0)
        grad_x = jnp.roll(corr, -1, axis=1) - jnp.roll(corr, 1, axis=1)
        total = corr + (0.5 * smooth_y) * grad_y + (0.5 * smooth_x) * grad_x
        out_ref[p] = total * (1.0 / edge)


def gradient_matrix(size, edge, up):
    row = lax.broadcasted_iota(jnp.int32, (size, size), 0)
    col = lax.broadcasted_iota(jnp.int32, (size, size), 1)
    out, source = (row, col) if up else (col, row)
    following = jnp.where(out == edge - 1, 0, out + 1)
    before = jnp.where(out == 0, edge - 1, out - 1)
    inside = out < edge
    plus = jnp.where(jnp.logical_and(inside, source == following), 0.5, 0.0)
    minus = jnp.where(jnp.logical_and(inside, source == before), 0.5, 0.0)
    return (plus - minus).astype(BF16)


def render_kernel(count, edge, strips_of, n_block, n_smooth, *refs):
    blocks, smooths = refs[:n_block], refs[n_block : n_block + n_smooth]
    out_ref, onehot, stacked = refs[n_block + n_smooth :]
    rows = count * edge
    part = rows // 4
    rest = edge - LANES
    wide = round_up(rows, LANES)
    me = lax.axis_index("strip")
    smooth = smooths[0][...]
    for other in smooths[1:]:
        smooth = smooth + other[...]
    lanes_all = smooth.shape[1]
    along_y = gradient_matrix(edge, edge, True)
    along_x = gradient_matrix(2 * LANES, edge, False)
    lane = lax.broadcasted_iota(jnp.int32, (part, LANES), 1)
    ones_lane = jnp.where(lane == rest, 1.0, 0.0)
    land = lax.broadcasted_iota(jnp.int32, (rows, LANES), 0).astype(F32)
    first_row = (me * rows).astype(F32)

    def place(message, strip, slot):
        mine = pltpu.roll(smooth, lanes_all - strip * count, 1)
        side = message[rows : rows + part, :].astype(F32)
        for p in range(count):
            halves = []
            for g in (2 * p, 2 * p + 1):
                left = message[g * part : (g + 1) * part, :].astype(F32)
                turned = pltpu.roll(side, (LANES - g * rest) % LANES, 1) if g else side
                halves.append(
                    jnp.concatenate([left, jnp.where(lane < rest, turned, ones_lane)], axis=1)
                )
            base = jnp.concatenate(halves, axis=0)
            base_low = base.astype(BF16)
            grad_y = product(along_y, base_low)
            grad_x = product(base_low, along_x)
            smooth_y, smooth_x = mine[0:1, p : p + 1], mine[1:2, p : p + 1]
            aligned = base + smooth_y * grad_y + smooth_x * grad_x
            stacked[slot * wide + p * edge : slot * wide + (p + 1) * edge, :] = aligned.astype(BF16)
        if wide > rows:
            stacked[slot * wide + rows : (slot + 1) * wide, :] = jnp.zeros(
                (wide - rows, 2 * LANES), BF16
            )
        tail = message[rows + part :, :].astype(F32)
        key = tail[0:8] * 256.0 + tail[8:16] - first_row
        for j in range(wide // LANES):
            onehot[:, slot * wide + j * LANES : slot * wide + (j + 1) * LANES] = jnp.where(
                land == key[j : j + 1, :], 1.0, 0.0
            ).astype(BF16)

    if len(blocks[0].shape) == 2:
        for slot, (block, offset) in enumerate(zip(blocks, strips_of)):
            place(block, jnp.bitwise_xor(me, offset), slot)
        total = product(onehot[...], stacked[...])
    else:

        def step(i, total):
            place(blocks[0].at[i], i, 0)
            return total + product(onehot[...], stacked[...])

        total = lax.fori_loop(0, blocks[0].shape[0], step, jnp.zeros((rows, 2 * LANES), F32))
    counts = jnp.maximum(total[:, edge : edge + 1], 1.0)
    out_ref[...] = (total[:, :edge] / counts).astype(BF16)


def turned(block, axis, distance):
    size = lax.axis_size(axis)
    return lax.ppermute(block, axis, [(i, (i + distance) % size) for i in range(size)])


def swapped(block, offset):
    return lax.ppermute(
        block, "strip", [(i, i ^ offset) for i in range(lax.axis_size("strip"))]
    )


def on_device(image, peaks, row_source, row_weight, col_source, col_weight, owner, render_row):
    pixels = image[0]
    count, edge, _ = pixels.shape
    rows = count * edge
    sections, strips = lax.axis_size("sec"), lax.axis_size("strip")
    dft_cos, dft_sin = dft_tables(edge)
    length = message_rows(rows)
    wide = round_up(rows, LANES)

    message = call(
        base_kernel,
        jax.ShapeDtypeStruct((length, LANES), BF16),
        7,
        scratch=[pltpu.VMEM((16, wide), F32)],
    )(
        pixels,
        row_source[0],
        row_weight[0],
        col_source[0],
        col_weight[0],
        owner[0].reshape(1, rows),
        render_row,
    )
    prior_message = turned(message, "sec", 1)
    table = jax.ShapeDtypeStruct((count, edge, edge), F32)
    img_re, img_im = call(spectrum_kernel, (table, table), 3)(pixels, dft_cos, dft_sin)
    corr, near = call(
        surface_kernel,
        (table, jax.ShapeDtypeStruct((8, LANES), F32)),
        6,
        smem=(5,),
        scratch=[pltpu.VMEM((count, edge + 8, edge), F32)],
    )(prior_message, img_re, img_im, dft_cos, dft_sin, peaks[0])

    few = strips <= 8 and strips & (strips - 1) == 0
    if few:
        offsets = [2 * k for k in range(strips // 2)]
        blocks = [message] + [swapped(message, offset) for offset in offsets[1:]]
        blocks = blocks + [swapped(block, 1) for block in blocks]
        offsets = offsets + [offset + 1 for offset in offsets]
    else:
        blocks, offsets = [lax.all_gather(message, "strip")], None

    nears = [near] + [turned(near, "sec", k) for k in range(1, sections - 1)]
    patches_all = round_up(count * strips, LANES)
    smooth, prior = call(
        functools.partial(chain_kernel, count, len(nears)),
        (
            jax.ShapeDtypeStruct((8, patches_all), F32),
            jax.ShapeDtypeStruct((8, LANES), F32),
        ),
        len(nears),
    )(*nears)
    corr_map = call(map_kernel, table, 2)(corr, prior)
    if few:
        total = smooth
        for offset in offsets[1 : strips // 2]:
            total = total + swapped(smooth, offset)
        smooths = [total, swapped(total, 1)]
    else:
        smooths = [lax.psum(smooth, "strip")]
    slots = len(blocks)
    render = call(
        functools.partial(render_kernel, count, edge, offsets, len(blocks), len(smooths)),
        jax.ShapeDtypeStruct((rows, edge), BF16),
        len(blocks) + len(smooths),
        scratch=[
            pltpu.VMEM((rows, slots * wide), BF16),
            pltpu.VMEM((slots * wide, 2 * LANES), BF16),
        ],
    )(*blocks, *smooths)
    return (render[None], corr_map[None])


def solution(mesh):
    placed = (
        P("sec", "strip", None, None),
        P("sec", "strip", None),
        P("sec", "strip", None),
        P("sec", "strip", None),
        P("sec", "strip", None),
        P("sec", "strip", None),
        P("sec", "strip", None),
        P("sec", "strip"),
    )
    return jax.shard_map(
        on_device,
        mesh=mesh,
        in_specs=placed,
        out_specs=(P("sec", "strip", None), P("sec", "strip", None, None)),
        check_vma=False,
    )
```

profile of v0, /device:TPU:0, one launch (start us, length us, event | category | flops | bytes accessed | tf_op | source)
XLA Modules:
  0.0 32.3 jit_solution(2494158236714967060)
XLA Ops:
  0.6 0.0 copy-start.7
  0.6 0.0 copy-start.8
  0.7 0.0 copy-start.6
  0.7 0.0 copy-start.5
  0.7 0.0 copy-start.4
  0.7 0.0 copy-start.3
  0.7 0.6 %copy-done.7 = s32[1,320,1]{1,2,0:T(1,128)S(1)} copy-done((s32[1,320,1]{1,2,0:T(1,128)S(1)}, s32[1,320,1]{1,2,0:T(1,128)}, u32[]{:S(2)}) %copy-start.7) | copy-done | bytes 1304
  1.3 0.0 copy-done.8
  1.3 0.0 copy-done.6
  1.3 0.0 copy-done.5
  1.4 0.0 copy-done.4
  1.4 0.0 copy-done.3
  1.4 0.0 copy-start
  1.4 0.9 %copy-done = bf16[1,2,160,160]{3,2,1,0:T(8,128)(2,1)S(1)} copy-done((bf16[1,2,160,160]{3,2,1,0:T(8,128)(2,1)S(1)}, bf16[1,2,160,160]{3,2,1,0:T(8,128)(2,1)}, u32[]{:S(2)}) %copy-start) | copy-done | bytes 102424
  2.3 0.0 copy-start.1
  2.3 0.0 copy-start.2
  2.3 0.5 %shard_map.113.refs_0_ = bf16[416,128]{1,0:T(8,128)(2,1)S(1)} custom-call(bf16[2,160,160]{2,1,0:T(8,128)(2,1)S(1)} %bitcast.10, s32[2,160]{1,0:T(2,128)S(1)} %bitcast.12, f32[2,160]{1,0:T(2,128)S(1)} %bitcast.13, s32[2,160]{1,0:T(2,128)S(1)} %bitcast.14, f32[2,160]{1,0:T(2,128)S(1)} %bitcast.15, s32[1,320]{1,0:T(1,128)S(1)} %bitcast.16, s32[1,320]{1,0:T(1,128)S(1)} %copy-done.8), custom_call_target="tpu_custom_call" | custom-call | flops 1000000 | bytes 500000 | tf_op jit(solution)/shard_map/pallas_call | solution.py:326
  2.8 3.0 %collective-permute-start.7 = (bf16[416,128]{1,0:T(8,128)(2,1)S(1)}, bf16[416,128]{1,0:T(8,128)(2,1)S(1)}, u32[]{:S(2)}, u32[]{:S(2)}) collective-permute-start(bf16[416,128]{1,0:T(8,128)(2,1)S(1)} %shard_map.113.refs_0_), channel_id=1, source_target_pairs={{0,8},{8,16},{16,24},{24,0},{1,9},{9,17},{17,25},{25,1},{2,10},{10... | collective-permute-start | bytes 319496 | tf_op jit(solution)/shard_map/ppermute | solution.py:308
  5.8 1.6 %collective-permute-start = (bf16[416,128]{1,0:T(8,128)(2,1)S(1)}, bf16[416,128]{1,0:T(8,128)(2,1)S(1)}, u32[]{:S(2)}, u32[]{:S(2)}) collective-permute-start(bf16[416,128]{1,0:T(8,128)(2,1)S(1)} %shard_map.113.refs_0_), channel_id=1, source_target_pairs={{0,2},{1,3},{2,0},{3,1},{4,6},{5,7},{6,4},{7,5},{8,10},{9,11},{10,... | collective-permute-start | bytes 319496 | tf_op jit(solution)/shard_map/ppermute | solution.py:312
  7.3 2.6 %collective-permute-start.1 = (bf16[416,128]{1,0:T(8,128)(2,1)S(1)}, bf16[416,128]{1,0:T(8,128)(2,1)S(1)}, u32[]{:S(2)}, u32[]{:S(2)}) collective-permute-start(bf16[416,128]{1,0:T(8,128)(2,1)S(1)} %shard_map.113.refs_0_), channel_id=1, source_target_pairs={{0,4},{1,5},{2,6},{3,7},{4,0},{5,1},{6,2},{7,3},{8,12},{9,13},{10,... | collective-permute-start | bytes 319496 | tf_op jit(solution)/shard_map/ppermute | solution.py:312
  9.9 0.2 collective-permute-start.2
  10.1 0.0 copy-done.1
  10.2 0.0 copy-done.2
  10.2 0.5 %shard_map.114 = (f32[2,160,160]{2,1,0:T(8,128)S(1)}, f32[2,160,160]{2,1,0:T(8,128)S(1)}) custom-call(bf16[2,160,160]{2,1,0:T(8,128)(2,1)S(1)} %bitcast.11, bf16[160,160]{1,0:T(8,128)(2,1)S(1)} %copy-done.1, bf16[160,160]{1,0:T(8,128)(2,1)S(1)} %copy-done.2), custom_call_target="tpu_custom_call" | custom-call | flops 1000000 | bytes 500000 | tf_op jit(solution)/shard_map/pallas_call | solution.py:342
  10.7 0.0 collective-permute-done.7.message_ref
  10.7 0.0 copy-start.9
  10.7 0.7 %copy-done.9 = s32[1,2,2]{2,1,0:T(2,128)S(1)} copy-done((s32[1,2,2]{2,1,0:T(2,128)S(1)}, s32[1,2,2]{2,1,0:T(2,128)}, u32[]{:S(2)}) %copy-start.9) | copy-done | bytes 40
  11.4 1.7 %shard_map.115 = (f32[2,160,160]{2,1,0:T(8,128)S(1)}, f32[8,128]{1,0:T(8,128)S(1)}) custom-call(bf16[416,128]{1,0:T(8,128)(2,1)S(1)} %collective-permute-done.7.message_ref, f32[2,160,160]{2,1,0:T(8,128)S(1)} %get-tuple-element.8.im_re_ref, f32[2,160,160]{2,1,0:T(8,128)S(1)} %get-tuple-element.9.im_im_ref, bf16[160,160]{1,0:T(8,128)(2,1)S(1)} %copy-done.1, ...), custom_call_target="tpu_custom_call" | custom-call | flops 1000000 | bytes 500000 | tf_op jit(solution)/shard_map/pallas_call | solution.py:343
  13.1 1.5 %collective-permute-start.8 = (f32[8,128]{1,0:T(8,128)S(1)}, f32[8,128]{1,0:T(8,128)S(1)}, u32[]{:S(2)}, u32[]{:S(2)}) collective-permute-start(f32[8,128]{1,0:T(8,128)S(1)} %get-tuple-element.10.refs_0_), channel_id=1, source_target_pairs={{0,8},{8,16},{16,24},{24,0},{1,9},{9,17},{17,25},{25,1},{2,10},{10... | collective-permute-start | bytes 12296 | tf_op jit(solution)/shard_map/ppermute | solution.py:308
  14.6 0.3 collective-permute-start.9
  14.8 2.7 %collective-permute-done.8.refs_1_ = f32[8,128]{1,0:T(8,128)S(1)} collective-permute-done((f32[8,128]{1,0:T(8,128)S(1)}, f32[8,128]{1,0:T(8,128)S(1)}, u32[]{:S(2)}, u32[]{:S(2)}) %collective-permute-start.8) | collective-permute-done | bytes 4128 | tf_op jit(solution)/shard_map/ppermute | solution.py:308
  17.6 0.6 %collective-permute-done.9.refs_2_ = f32[8,128]{1,0:T(8,128)S(1)} collective-permute-done((f32[8,128]{1,0:T(8,128)S(1)}, f32[8,128]{1,0:T(8,128)S(1)}, u32[]{:S(2)}, u32[]{:S(2)}) %collective-permute-start.9) | collective-permute-done | bytes 4128 | tf_op jit(solution)/shard_map/ppermute | solution.py:308
  18.2 0.6 %shard_map.116 = (f32[8,128]{1,0:T(8,128)S(1)}, f32[8,128]{1,0:T(8,128)S(1)}) custom-call(f32[8,128]{1,0:T(8,128)S(1)} %get-tuple-element.10.refs_0_, f32[8,128]{1,0:T(8,128)S(1)} %collective-permute-done.8.refs_1_, f32[8,128]{1,0:T(8,128)S(1)} %collective-permute-done.9.refs_2_), custom_call_target="tpu_custom_call" | custom-call | flops 1000000 | bytes 500000 | tf_op jit(solution)/shard_map/pallas_call | solution.py:362
  18.7 0.7 %collective-permute-start.10 = (f32[8,128]{1,0:T(8,128)S(1)}, f32[8,128]{1,0:T(8,128)S(1)}, u32[]{:S(2)}, u32[]{:S(2)}) collective-permute-start(f32[8,128]{1,0:T(8,128)S(1)} %get-tuple-element.11), channel_id=1, source_target_pairs={{0,2},{1,3},{2,0},{3,1},{4,6},{5,7},{6,4},{7,5},{8,10},{9,11},{10,... | collective-permute-start | bytes 12296 | tf_op jit(solution)/shard_map/ppermute | solution.py:312
  19.5 3.5 %collective-permute-start.11 = (f32[8,128]{1,0:T(8,128)S(1)}, f32[8,128]{1,0:T(8,128)S(1)}, u32[]{:S(2)}, u32[]{:S(2)}) collective-permute-start(f32[8,128]{1,0:T(8,128)S(1)} %get-tuple-element.11), channel_id=1, source_target_pairs={{0,4},{1,5},{2,6},{3,7},{4,0},{5,1},{6,2},{7,3},{8,12},{9,13},{10,... | collective-permute-start | bytes 12296 | tf_op jit(solution)/shard_map/ppermute | solution.py:312
  23.0 0.0 collective-permute-done.refs_1_
  23.0 0.2 collective-permute-start.12
  23.2 0.0 collective-permute-done.1.refs_2_
  23.2 0.0 collective-permute-start.3
  23.2 0.0 collective-permute-done.2.refs_3_
  23.2 0.5 %collective-permute-start.4 = (bf16[416,128]{1,0:T(8,128)(2,1)S(1)}, bf16[416,128]{1,0:T(8,128)(2,1)S(1)}, u32[]{:S(2)}, u32[]{:S(2)}) collective-permute-start(bf16[416,128]{1,0:T(8,128)(2,1)S(1)} %collective-permute-done.refs_1_), channel_id=1, source_target_pairs={{0,1},{1,0},{2,3},{3,2},{4,5},{5,4},{6,7},{7,6},{8,9},{9,8},{10,11... | collective-permute-start | bytes 319496 | tf_op jit(solution)/shard_map/ppermute | solution.py:312
  23.7 0.0 collective-permute-done.10
  23.7 0.1 collective-permute-start.5
  23.8 0.8 %collective-permute-done.11 = f32[8,128]{1,0:T(8,128)S(1)} collective-permute-done((f32[8,128]{1,0:T(8,128)S(1)}, f32[8,128]{1,0:T(8,128)S(1)}, u32[]{:S(2)}, u32[]{:S(2)}) %collective-permute-start.11) | collective-permute-done | bytes 4128 | tf_op jit(solution)/shard_map/ppermute | solution.py:312
  24.6 0.0 collective-permute-start.6
  24.6 3.8 %collective-permute-done.12 = f32[8,128]{1,0:T(8,128)S(1)} collective-permute-done((f32[8,128]{1,0:T(8,128)S(1)}, f32[8,128]{1,0:T(8,128)S(1)}, u32[]{:S(2)}, u32[]{:S(2)}) %collective-permute-start.12) | collective-permute-done | bytes 4128 | tf_op jit(solution)/shard_map/ppermute | solution.py:312
  28.4 0.0 collective-permute-start.13
  28.4 1.1 %shard_map.118 = f32[2,160,160]{2,1,0:T(8,128)} custom-call(f32[2,160,160]{2,1,0:T(8,128)S(1)} %get-tuple-element.12.corr_ref, f32[8,128]{1,0:T(8,128)S(1)} %get-tuple-element.13.prior_ref), custom_call_target="tpu_custom_call" | custom-call | flops 1000000 | bytes 500000 | tf_op jit(solution)/shard_map/pallas_call | solution.py:370
  29.5 0.0 collective-permute-done.3.refs_4_
  29.5 0.1 collective-permute-done.13.refs_9_
  29.6 0.0 collective-permute-done.4.refs_5_
  29.6 0.0 collective-permute-done.5.refs_6_
  29.6 0.0 collective-permute-done.6.refs_7_
  29.6 1.9 %shard_map.117 = bf16[320,160]{1,0:T(8,128)(2,1)S(1)} custom-call(bf16[416,128]{1,0:T(8,128)(2,1)S(1)} %shard_map.113.refs_0_, bf16[416,128]{1,0:T(8,128)(2,1)S(1)} %collective-permute-done.refs_1_, bf16[416,128]{1,0:T(8,128)(2,1)S(1)} %collective-permute-done.1.refs_2_, bf16[416,128]{1,0:T(8,128)(2,1)S(1)} %collective-permute-done.2.refs_3_, ...), custom_call_target="tpu_custom_call" | custom-call | flops 1000000 | bytes 500000 | tf_op jit(solution)/shard_map/pallas_call | solution.py:379
  31.5 0.8 %copy.12 = bf16[1,320,160]{1,2,0:T(8,128)(2,1)} copy(bf16[1,320,160]{2,1,0:T(8,128)(2,1)S(1)} %bitcast.9) | data formatting | bytes 204800
  (1 shorter events, 0.0 us)
Async XLA Ops:
  0.6 0.7 %copy-start.7 = (s32[1,320,1]{1,2,0:T(1,128)S(1)}, s32[1,320,1]{1,2,0:T(1,128)}, u32[]{:S(2)}) copy-start(s32[1,320,1]{1,2,0:T(1,128)} %param.16) | copy-start | bytes 3844
  0.6 0.7 %copy-start.8 = (s32[1,320]{1,0:T(1,128)S(1)}, s32[1,320]{1,0:T(1,128)}, u32[]{:S(2)}) copy-start(s32[1,320]{1,0:T(1,128)} %target_ref.1) | copy-start | bytes 3844
  0.7 0.7 %copy-start.6 = (f32[1,2,160]{2,1,0:T(2,128)S(1)}, f32[1,2,160]{2,1,0:T(2,128)}, u32[]{:S(2)}) copy-start(f32[1,2,160]{2,1,0:T(2,128)} %param.15) | copy-start | bytes 3844
  0.7 0.7 %copy-start.5 = (s32[1,2,160]{2,1,0:T(2,128)S(1)}, s32[1,2,160]{2,1,0:T(2,128)}, u32[]{:S(2)}) copy-start(s32[1,2,160]{2,1,0:T(2,128)} %param.14) | copy-start | bytes 3844
  0.7 0.7 %copy-start.4 = (f32[1,2,160]{2,1,0:T(2,128)S(1)}, f32[1,2,160]{2,1,0:T(2,128)}, u32[]{:S(2)}) copy-start(f32[1,2,160]{2,1,0:T(2,128)} %param.13) | copy-start | bytes 3844
  0.7 0.7 %copy-start.3 = (s32[1,2,160]{2,1,0:T(2,128)S(1)}, s32[1,2,160]{2,1,0:T(2,128)}, u32[]{:S(2)}) copy-start(s32[1,2,160]{2,1,0:T(2,128)} %param.12) | copy-start | bytes 3844
  1.4 0.9 %copy-start = (bf16[1,2,160,160]{3,2,1,0:T(8,128)(2,1)S(1)}, bf16[1,2,160,160]{3,2,1,0:T(8,128)(2,1)}, u32[]{:S(2)}) copy-start(bf16[1,2,160,160]{3,2,1,0:T(8,128)(2,1)} %param.10) | copy-start | bytes 307204
  2.3 7.8 %copy-start.1 = (bf16[160,160]{1,0:T(8,128)(2,1)S(1)}, bf16[160,160]{1,0:T(8,128)(2,1)}, u32[]{:S(2)}) copy-start(bf16[160,160]{1,0:T(8,128)(2,1)} %constant.4.clone.cos_ref) | copy-start | bytes 153604
  2.3 7.8 %copy-start.2 = (bf16[160,160]{1,0:T(8,128)(2,1)S(1)}, bf16[160,160]{1,0:T(8,128)(2,1)}, u32[]{:S(2)}) copy-start(bf16[160,160]{1,0:T(8,128)(2,1)} %constant.5.clone.sin_ref) | copy-start | bytes 153604
  2.8 7.9 %collective-permute-start.7 = (bf16[416,128]{1,0:T(8,128)(2,1)S(1)}, bf16[416,128]{1,0:T(8,128)(2,1)S(1)}, u32[]{:S(2)}, u32[]{:S(2)}) collective-permute-start(bf16[416,128]{1,0:T(8,128)(2,1)S(1)} %shard_map.113.refs_0_), channel_id=1, source_target_pairs={{0,8},{8,16},{16,24},{24,0},{1,9},{9,17},{17,25},{25,1},{2,10},{10... | collective-permute-start | bytes 319496 | tf_op jit(solution)/shard_map/ppermute | solution.py:308
  5.8 17.2 %collective-permute-start = (bf16[416,128]{1,0:T(8,128)(2,1)S(1)}, bf16[416,128]{1,0:T(8,128)(2,1)S(1)}, u32[]{:S(2)}, u32[]{:S(2)}) collective-permute-start(bf16[416,128]{1,0:T(8,128)(2,1)S(1)} %shard_map.113.refs_0_), channel_id=1, source_target_pairs={{0,2},{1,3},{2,0},{3,1},{4,6},{5,7},{6,4},{7,5},{8,10},{9,11},{10,... | collective-permute-start | bytes 319496 | tf_op jit(solution)/shard_map/ppermute | solution.py:312
  7.3 15.9 %collective-permute-start.1 = (bf16[416,128]{1,0:T(8,128)(2,1)S(1)}, bf16[416,128]{1,0:T(8,128)(2,1)S(1)}, u32[]{:S(2)}, u32[]{:S(2)}) collective-permute-start(bf16[416,128]{1,0:T(8,128)(2,1)S(1)} %shard_map.113.refs_0_), channel_id=1, source_target_pairs={{0,4},{1,5},{2,6},{3,7},{4,0},{5,1},{6,2},{7,3},{8,12},{9,13},{10,... | collective-permute-start | bytes 319496 | tf_op jit(solution)/shard_map/ppermute | solution.py:312
  9.9 13.3 %collective-permute-start.2 = (bf16[416,128]{1,0:T(8,128)(2,1)S(1)}, bf16[416,128]{1,0:T(8,128)(2,1)S(1)}, u32[]{:S(2)}, u32[]{:S(2)}) collective-permute-start(bf16[416,128]{1,0:T(8,128)(2,1)S(1)} %shard_map.113.refs_0_), channel_id=1, source_target_pairs={{0,6},{1,7},{2,4},{3,5},{4,2},{5,3},{6,0},{7,1},{8,14},{9,15},{10,... | collective-permute-start | bytes 319496 | tf_op jit(solution)/shard_map/ppermute | solution.py:312
  10.7 0.7 %copy-start.9 = (s32[1,2,2]{2,1,0:T(2,128)S(1)}, s32[1,2,2]{2,1,0:T(2,128)}, u32[]{:S(2)}) copy-start(s32[1,2,2]{2,1,0:T(2,128)} %param.11) | copy-start | bytes 52
  13.1 4.5 %collective-permute-start.8 = (f32[8,128]{1,0:T(8,128)S(1)}, f32[8,128]{1,0:T(8,128)S(1)}, u32[]{:S(2)}, u32[]{:S(2)}) collective-permute-start(f32[8,128]{1,0:T(8,128)S(1)} %get-tuple-element.10.refs_0_), channel_id=1, source_target_pairs={{0,8},{8,16},{16,24},{24,0},{1,9},{9,17},{17,25},{25,1},{2,10},{10... | collective-permute-start | bytes 12296 | tf_op jit(solution)/shard_map/ppermute | solution.py:308
  14.6 3.6 %collective-permute-start.9 = (f32[8,128]{1,0:T(8,128)S(1)}, f32[8,128]{1,0:T(8,128)S(1)}, u32[]{:S(2)}, u32[]{:S(2)}) collective-permute-start(f32[8,128]{1,0:T(8,128)S(1)} %get-tuple-element.10.refs_0_), channel_id=1, source_target_pairs={{0,16},{8,24},{16,0},{24,8},{1,17},{9,25},{17,1},{25,9},{2,18},{10... | collective-permute-start | bytes 12296 | tf_op jit(solution)/shard_map/ppermute | solution.py:308
  18.7 5.0 %collective-permute-start.10 = (f32[8,128]{1,0:T(8,128)S(1)}, f32[8,128]{1,0:T(8,128)S(1)}, u32[]{:S(2)}, u32[]{:S(2)}) collective-permute-start(f32[8,128]{1,0:T(8,128)S(1)} %get-tuple-element.11), channel_id=1, source_target_pairs={{0,2},{1,3},{2,0},{3,1},{4,6},{5,7},{6,4},{7,5},{8,10},{9,11},{10,... | collective-permute-start | bytes 12296 | tf_op jit(solution)/shard_map/ppermute | solution.py:312
  19.5 5.1 %collective-permute-start.11 = (f32[8,128]{1,0:T(8,128)S(1)}, f32[8,128]{1,0:T(8,128)S(1)}, u32[]{:S(2)}, u32[]{:S(2)}) collective-permute-start(f32[8,128]{1,0:T(8,128)S(1)} %get-tuple-element.11), channel_id=1, source_target_pairs={{0,4},{1,5},{2,6},{3,7},{4,0},{5,1},{6,2},{7,3},{8,12},{9,13},{10,... | collective-permute-start | bytes 12296 | tf_op jit(solution)/shard_map/ppermute | solution.py:312
  23.0 5.4 %collective-permute-start.12 = (f32[8,128]{1,0:T(8,128)S(1)}, f32[8,128]{1,0:T(8,128)S(1)}, u32[]{:S(2)}, u32[]{:S(2)}) collective-permute-start(f32[8,128]{1,0:T(8,128)S(1)} %get-tuple-element.11), channel_id=1, source_target_pairs={{0,6},{1,7},{2,4},{3,5},{4,2},{5,3},{6,0},{7,1},{8,14},{9,15},{10,... | collective-permute-start | bytes 12296 | tf_op jit(solution)/shard_map/ppermute | solution.py:312
  23.2 6.3 %collective-permute-start.3 = (bf16[416,128]{1,0:T(8,128)(2,1)S(1)}, bf16[416,128]{1,0:T(8,128)(2,1)S(1)}, u32[]{:S(2)}, u32[]{:S(2)}) collective-permute-start(bf16[416,128]{1,0:T(8,128)(2,1)S(1)} %shard_map.113.refs_0_), channel_id=1, source_target_pairs={{0,1},{1,0},{2,3},{3,2},{4,5},{5,4},{6,7},{7,6},{8,9},{9,8},{10,11... | collective-permute-start | bytes 319496 | tf_op jit(solution)/shard_map/ppermute | solution.py:312
  23.2 6.4 %collective-permute-start.4 = (bf16[416,128]{1,0:T(8,128)(2,1)S(1)}, bf16[416,128]{1,0:T(8,128)(2,1)S(1)}, u32[]{:S(2)}, u32[]{:S(2)}) collective-permute-start(bf16[416,128]{1,0:T(8,128)(2,1)S(1)} %collective-permute-done.refs_1_), channel_id=1, source_target_pairs={{0,1},{1,0},{2,3},{3,2},{4,5},{5,4},{6,7},{7,6},{8,9},{9,8},{10,11... | collective-permute-start | bytes 319496 | tf_op jit(solution)/shard_map/ppermute | solution.py:312
  23.7 5.8 %collective-permute-start.5 = (bf16[416,128]{1,0:T(8,128)(2,1)S(1)}, bf16[416,128]{1,0:T(8,128)(2,1)S(1)}, u32[]{:S(2)}, u32[]{:S(2)}) collective-permute-start(bf16[416,128]{1,0:T(8,128)(2,1)S(1)} %collective-permute-done.1.refs_2_), channel_id=1, source_target_pairs={{0,1},{1,0},{2,3},{3,2},{4,5},{5,4},{6,7},{7,6},{8,9},{9,8},{10,11... | collective-permute-start | bytes 319496 | tf_op jit(solution)/shard_map/ppermute | solution.py:312
  24.6 5.0 %collective-permute-start.6 = (bf16[416,128]{1,0:T(8,128)(2,1)S(1)}, bf16[416,128]{1,0:T(8,128)(2,1)S(1)}, u32[]{:S(2)}, u32[]{:S(2)}) collective-permute-start(bf16[416,128]{1,0:T(8,128)(2,1)S(1)} %collective-permute-done.2.refs_3_), channel_id=1, source_target_pairs={{0,1},{1,0},{2,3},{3,2},{4,5},{5,4},{6,7},{7,6},{8,9},{9,8},{10,11... | collective-permute-start | bytes 319496 | tf_op jit(solution)/shard_map/ppermute | solution.py:312
  28.4 1.2 %collective-permute-start.13 = (f32[8,128]{1,0:T(8,128)S(1)}, f32[8,128]{1,0:T(8,128)S(1)}, u32[]{:S(2)}, u32[]{:S(2)}) collective-permute-start(f32[8,128]{1,0:T(8,128)S(1)} %add_add_fusion.refs_8_), channel_id=1, source_target_pairs={{0,1},{1,0},{2,3},{3,2},{4,5},{5,4},{6,7},{7,6},{8,9},{9,8},{10,11... | collective-permute-start | bytes 12296 | tf_op jit(solution)/shard_map/ppermute | solution.py:312
where the time goes:
time: 32.5 us; the launch traced here: 32.3 us
  starting transfers between devices  14.2 us (44%)
  waiting for transfers between devices  7.98 us (25%)
  Pallas kernels  6.24 us (19%)
  local copies, waits for them, and re-layouts  3.07 us (9%)
  between operations  0.75 us (2%)
    ppermute x11, starting transfers between devices, swapped(): lax.ppermute(block, 'strip', [(i, i ^ offset) for i in range(lax.axis_siz...  9.42 us
    ppermute x3, starting transfers between devices, turned(): lax.ppermute(block, axis, [(i, (i + distance) % size) for i in range(size)])  4.78 us
    ppermute x11, waiting for transfers between devices, swapped(): lax.ppermute(block, 'strip', [(i, i ^ offset) for i in range(lax.axis_siz...  4.66 us
    ppermute x3, waiting for transfers between devices, turned(): lax.ppermute(block, axis, [(i, (i + distance) % size) for i in range(size)])  3.32 us
    unnamed x21, local copies, waits for them, and re-layouts  3.07 us
    pallas_call x1, Pallas kernels, on_device(): call(functools.partial(render_kernel, count, edge, offsets, len(blocks),...  1.92 us
    pallas_call x1, Pallas kernels, on_device(): call(surface_kernel, (table, jax.ShapeDtypeStruct((8, LANES), F32)), 6, s...  1.7 us
    pallas_call x1, Pallas kernels, on_device(): corr_map = call(map_kernel, table, 2)(corr, prior)  1.11 us
  transfers between devices with their start and end apart: 14, of which 4 were waited for; matrix products, arithmetic and copies ran while one was open for 0% of the time, Pallas kernels for 12%

commit v1 on v0

v1 whole, which is shorter than its diff:
```python
import functools

import jax
import jax.numpy as jnp
import numpy as np
from jax import lax
from jax.experimental import pallas as pl
from jax.experimental.pallas import tpu as pltpu
from jax.sharding import PartitionSpec as P

GC = 2
LANES = 128
TWO_PI = 2.0 * 3.141592653589793
F32 = jnp.float32
BF16 = jnp.bfloat16
VMEM_BYTES = 16 * 1024 * 1024


def product(left, right):
    return jnp.dot(left, right, preferred_element_type=F32)


def dft_tables(edge):
    positions = np.arange(edge, dtype=np.int32)
    phases = positions[:, None] * positions[None, :] % edge
    angles = phases.astype(np.float32) * np.float32(TWO_PI / edge)
    return jnp.asarray(np.cos(angles), BF16), jnp.asarray(np.sin(angles), BF16)


def round_up(size, unit):
    return -(-size // unit) * unit


def message_rows(rows):
    return rows + rows // 4 + 16


def call(kernel, out_shape, n_in, space=pltpu.VMEM, scratch=(), vmem=VMEM_BYTES, flops=1000000000):
    specs = [pl.BlockSpec(memory_space=space) for _ in range(n_in)]
    outs = jax.tree.map(lambda _: pl.BlockSpec(memory_space=pltpu.VMEM), out_shape)
    return pl.pallas_call(
        kernel,
        out_shape=out_shape,
        in_specs=specs,
        out_specs=outs,
        scratch_shapes=list(scratch),
        compiler_params=pltpu.CompilerParams(vmem_limit_bytes=vmem),
        cost_estimate=pl.CostEstimate(flops=flops, bytes_accessed=500000, transcendentals=0),
    )


def warp_matrix_t(source, weight, edge):
    spots = lax.broadcasted_iota(jnp.int32, (edge, edge), 0)
    following = jnp.where(source == edge - 1, 0, source + 1)
    first = jnp.where(spots == source, weight, 0.0)
    second = jnp.where(spots == following, 1.0 - weight, 0.0)
    return (first + second).astype(BF16)


def base_kernel(*refs):
    sources, out_ref, targets, (keys, sems) = refs[:7], refs[7], refs[8:15], refs[15:]
    copies = [
        pltpu.make_async_copy(source, target, sems.at[i])
        for i, (source, target) in enumerate(zip(sources, targets))
    ]
    for copy in copies:
        copy.start()
    image_ref, row_src, row_wt, col_src, col_wt, owner_ref, target_ref = targets
    for copy in copies[1:]:
        copy.wait()
    count, edge, _ = image_ref.shape
    rows = count * edge
    part = rows // 4
    keys[...] = jnp.full(keys.shape, -1.0, F32)
    row_ts, col_ts = [], []
    for p in range(count):
        row_ts.append(warp_matrix_t(row_src[p : p + 1, :], row_wt[p : p + 1, :], edge))
        col_ts.append(warp_matrix_t(col_src[p : p + 1, :], col_wt[p : p + 1, :], edge))
    key = owner_ref[...] * rows + target_ref[...]
    keys[0:1, 0:rows] = (key >> 8).astype(F32)
    keys[8:9, 0:rows] = (key & 255).astype(F32)
    wide = keys.shape[1] // LANES
    blank = jnp.full((8 - wide, LANES), -1.0, F32)
    lines = []
    for half in (0, 8):
        lines += [keys[half : half + 1, j * LANES : (j + 1) * LANES] for j in range(wide)]
        lines += [blank]
    out_ref[rows + part :, :] = jnp.concatenate(lines, axis=0).astype(BF16)
    copies[0].wait()
    pieces = []
    for p in range(count):
        row_warped = lax.dot_general(
            row_ts[p], image_ref[p], (((0,), (0,)), ((), ())), preferred_element_type=F32
        ).astype(BF16)
        base = product(row_warped, col_ts[p])
        out_ref[p * edge : (p + 1) * edge, :] = base[:, :LANES].astype(BF16)
        right = base[:, LANES:]
        pieces += [right[:part], right[part:]]
    out_ref[rows : rows + part, :] = jnp.concatenate(pieces, axis=1).astype(BF16)


def spectrum_of(pixels, dft_cos, dft_sin, count, edge):
    half_re = product(pixels, dft_cos).astype(BF16)
    half_im = (-product(pixels, dft_sin)).astype(BF16)
    spectra = []
    for p in range(count):
        h_re = half_re[p * edge : (p + 1) * edge]
        h_im = half_im[p * edge : (p + 1) * edge]
        spectra.append(
            (
                product(dft_cos, h_re) + product(dft_sin, h_im),
                product(dft_cos, h_im) - product(dft_sin, h_re),
            )
        )
    return spectra


def spectrum_kernel(
    image_ref,
    cos_ref,
    sin_ref,
    peaks_ref,
    message_ref,
    re_ref,
    im_ref,
    cos_row,
    sin_row,
    cos_col,
    sin_col,
    copied_ref,
):
    count, edge, _ = image_ref.shape
    copied_ref[...] = message_ref[...]
    dft_cos, dft_sin = cos_ref[...], sin_ref[...]
    pixels = image_ref[...].reshape(count * edge, edge)
    spectra = spectrum_of(pixels, dft_cos, dft_sin, count, edge)
    for p, (s_re, s_im) in enumerate(spectra):
        re_ref[p] = s_re
        im_ref[p] = s_im

    def wrap(spot):
        return jnp.where(spot < 0, spot + edge, jnp.where(spot >= edge, spot - edge, spot))

    row = lax.broadcasted_iota(jnp.int32, (16, edge), 0)
    row_lane = lax.broadcasted_iota(jnp.int32, (16, edge), 1)
    col = lax.broadcasted_iota(jnp.int32, (edge, LANES), 0)
    col_lane = lax.broadcasted_iota(jnp.int32, (edge, LANES), 1)
    for p in range(count):
        spot = wrap(peaks_ref[p : p + 1, 0:1] + (row - 2))
        pick = jnp.where(jnp.logical_and(row < 5, row_lane == spot), 1.0, 0.0).astype(BF16)
        cos_row[p] = product(pick, dft_cos).astype(BF16)
        sin_row[p] = product(pick, dft_sin).astype(BF16)
        step = col_lane - (8 * p + 2)
        spot = wrap(peaks_ref[p : p + 1, 1:2] + step)
        near = jnp.logical_and(step >= -2, step <= 2)
        pick = jnp.where(jnp.logical_and(near, col == spot), 1.0, 0.0).astype(BF16)
        cos_col[p] = product(dft_cos, pick).astype(BF16)
        sin_col[p] = product(dft_sin, pick).astype(BF16)


def near_kernel(
    message_ref,
    im_re_ref,
    im_im_ref,
    cos_ref,
    sin_ref,
    cos_row,
    sin_row,
    cos_col,
    sin_col,
    near_ref,
    cross_re_ref,
    cross_im_ref,
):
    count, edge, _ = im_re_ref.shape
    rows = count * edge
    part = rows // 4
    rest = edge - LANES
    dft_cos, dft_sin = cos_ref[...], sin_ref[...]
    side = message_ref[rows : rows + part, :].astype(F32)
    groups = []
    for g in range(4):
        left = message_ref[g * part : (g + 1) * part, :].astype(F32)
        groups.append(jnp.concatenate([left, side[:, g * rest : (g + 1) * rest]], axis=1))
    pixels = jnp.concatenate(groups, axis=0)
    pixels = jnp.where(lax.axis_index("sec") > 0, pixels, 0.0).astype(BF16)
    spectra = spectrum_of(pixels, dft_cos, dft_sin, count, edge)
    total = None
    for p, (ref_re, ref_im) in enumerate(spectra):
        img_re, img_im = im_re_ref[p], im_im_ref[p]
        cross_re = (ref_re * img_re + ref_im * img_im).astype(BF16)
        cross_im = (ref_im * img_re - ref_re * img_im).astype(BF16)
        cross_re_ref[p] = cross_re
        cross_im_ref[p] = cross_im
        back_re = (product(cross_re, cos_col[p]) - product(cross_im, sin_col[p])).astype(BF16)
        back_im = (product(cross_re, sin_col[p]) + product(cross_im, cos_col[p])).astype(BF16)
        near = product(cos_row[p], back_re) - product(sin_row[p], back_im)
        total = near if total is None else total + near
    near_ref[...] = total[0:8] * (1.0 / (edge * edge))


def chain_kernel(count, steps, *refs):
    near_refs, (smooth_ref, prior_ref) = refs[:steps], refs[-2:]
    section = lax.axis_index("sec")
    strip = lax.axis_index("strip")
    row = lax.broadcasted_iota(jnp.int32, (8, LANES), 0)
    lane = lax.broadcasted_iota(jnp.int32, (8, LANES), 1)

    def spread(values):
        tile = jnp.broadcast_to(values[0], (8, LANES))
        for p in range(1, count):
            tile = jnp.where(lane >= 8 * p, values[p], tile)
        return tile

    zeros = [jnp.zeros((1, 1), F32)] * count
    smooth_y, smooth_x = zeros, zeros
    for back in range(steps - 1, -1, -1):
        prior_y, prior_x = smooth_y, smooth_x
        near = near_refs[back][...]
        grad_y = 0.5 * (pltpu.roll(near, 7, 0) - pltpu.roll(near, 1, 0))
        grad_x = 0.5 * (pltpu.roll(near, LANES - 1, 1) - pltpu.roll(near, 1, 1))
        corr = near + spread(prior_y) * grad_y + spread(prior_x) * grad_x
        size = jnp.abs(corr)
        below, above = pltpu.roll(corr, 7, 0), pltpu.roll(corr, 1, 0)
        right, left = pltpu.roll(corr, LANES - 1, 1), pltpu.roll(corr, 1, 1)
        flow_y = (below - above) / (jnp.abs(below) + size + jnp.abs(above) + 1.0)
        flow_x = (right - left) / (jnp.abs(right) + size + jnp.abs(left) + 1.0)

        def picked(flow):
            values = []
            for p in range(count):
                here = jnp.logical_and(row == 2, lane == 8 * p + 2)
                spot = jnp.where(here, flow, 0.0)
                values.append(jnp.sum(jnp.sum(spot, axis=1, keepdims=True), axis=0, keepdims=True))
            smooth = []
            for p in range(count):
                total = 0.5 * values[p]
                if p % GC > 0:
                    total = total + 0.25 * values[p - 1]
                if p % GC < GC - 1:
                    total = total + 0.25 * values[p + 1]
                smooth.append(jnp.where(section - back > 0, total, 0.0))
            return smooth

        smooth_y, smooth_x = picked(flow_y), picked(flow_x)

    def laid(values_y, values_x, shape, first):
        out_row = lax.broadcasted_iota(jnp.int32, shape, 0)
        out_lane = lax.broadcasted_iota(jnp.int32, shape, 1)
        tile = jnp.zeros(shape, F32)
        for p in range(count):
            pair = jnp.where(out_row == 0, values_y[p], values_x[p])
            here = jnp.logical_and(out_lane == first + p, out_row < 2)
            tile = jnp.where(here, pair, tile)
        return tile

    smooth_ref[...] = laid(smooth_y, smooth_x, smooth_ref.shape, strip * count)
    prior_ref[...] = laid(prior_y, prior_x, prior_ref.shape, 0)


def surface_kernel(cross_re_ref, cross_im_ref, cos_ref, sin_ref, corr_ref, grad_y_ref, grad_x_ref):
    count, edge, _ = cross_re_ref.shape
    dft_cos, dft_sin = cos_ref[...], sin_ref[...]
    for p in range(count):
        cross_re, cross_im = cross_re_ref[p], cross_im_ref[p]
        back_re = (product(cross_re, dft_cos) - product(cross_im, dft_sin)).astype(BF16)
        back_im = (product(cross_re, dft_sin) + product(cross_im, dft_cos)).astype(BF16)
        corr = product(dft_cos, back_re) - product(dft_sin, back_im)
        corr = corr * (1.0 / (edge * edge * edge))
        corr_ref[p] = corr
        grad_y_ref[p] = 0.5 * (jnp.roll(corr, -1, axis=0) - jnp.roll(corr, 1, axis=0))
        grad_x_ref[p] = 0.5 * (jnp.roll(corr, -1, axis=1) - jnp.roll(corr, 1, axis=1))


def map_kernel(corr_ref, grad_y_ref, grad_x_ref, prior_ref, smooth_ref, out_ref, passed_ref):
    passed_ref[...] = smooth_ref[...]
    for p in range(corr_ref.shape[0]):
        smooth_y = prior_ref[0:1, p : p + 1]
        smooth_x = prior_ref[1:2, p : p + 1]
        out_ref[p] = corr_ref[p] + smooth_y * grad_y_ref[p] + smooth_x * grad_x_ref[p]


def gradient_matrix(size, edge, up):
    row = lax.broadcasted_iota(jnp.int32, (size, size), 0)
    col = lax.broadcasted_iota(jnp.int32, (size, size), 1)
    out, source = (row, col) if up else (col, row)
    following = jnp.where(out == edge - 1, 0, out + 1)
    before = jnp.where(out == 0, edge - 1, out - 1)
    inside = out < edge
    plus = jnp.where(jnp.logical_and(inside, source == following), 0.5, 0.0)
    minus = jnp.where(jnp.logical_and(inside, source == before), 0.5, 0.0)
    return (plus - minus).astype(BF16)


def lay_out(messages, count, edge, keys, onehot, base_out, grad_y_out, grad_x_out):
    rows = count * edge
    part = rows // 4
    rest = edge - LANES
    deep = onehot.shape[1]
    used = len(messages) * rows
    along_y = gradient_matrix(edge, edge, True)
    along_x = gradient_matrix(2 * LANES, edge, False)
    lane = lax.broadcasted_iota(jnp.int32, (part, LANES), 1)
    ones_lane = jnp.where(lane == rest, 1.0, 0.0)
    land = lax.broadcasted_iota(jnp.int32, (rows, LANES), 0).astype(F32)
    first_row = (lax.axis_index("strip") * rows).astype(F32)
    if deep > used:
        keys[...] = jnp.full(keys.shape, -1.0, F32)
        base_out[used:, :] = jnp.zeros((deep - used, 2 * LANES), BF16)
    for slot, message in enumerate(messages):
        side = message[rows : rows + part, :].astype(F32)
        for p in range(count):
            halves = []
            for g in (2 * p, 2 * p + 1):
                left = message[g * part : (g + 1) * part, :].astype(F32)
                turned_side = pltpu.roll(side, (LANES - g * rest) % LANES, 1) if g else side
                halves.append(
                    jnp.concatenate([left, jnp.where(lane < rest, turned_side, ones_lane)], axis=1)
                )
            base = jnp.concatenate(halves, axis=0).astype(BF16)
            place = slice(slot * rows + p * edge, slot * rows + (p + 1) * edge)
            base_out[place, :] = base
            grad_y_out[place, :] = product(along_y, base).astype(BF16)
            grad_x_out[place, :] = product(base, along_x).astype(BF16)
        tail = message[rows + part :, :].astype(F32)
        key = tail[0:8] * 256.0 + tail[8:16] - first_row
        for j in range(0, rows, LANES):
            size = min(LANES, rows - j)
            line = key[j // LANES : j // LANES + 1, :size]
            keys[0:1, slot * rows + j : slot * rows + j + size] = line
    for j in range(0, deep, LANES):
        hit = land == keys[0:1, j : j + LANES]
        onehot[:, j : j + LANES] = jnp.where(hit, 1.0, 0.0).astype(BF16)


def align_rows(smooth, strip, count, edge, slot, base_in, grad_y_in, grad_x_in, stacked):
    mine = pltpu.roll(smooth, smooth.shape[1] - strip * count, 1)
    for p in range(count):
        place = slice(slot * count * edge + p * edge, slot * count * edge + (p + 1) * edge)
        smooth_y = jnp.broadcast_to(mine[0:1, p : p + 1], (edge, 2 * LANES)).astype(BF16)
        smooth_x = jnp.broadcast_to(mine[1:2, p : p + 1], (edge, 2 * LANES)).astype(BF16)
        change = smooth_y * grad_y_in[place, :] + smooth_x * grad_x_in[place, :]
        stacked[place, :] = base_in[place, :] + change


def averaged(total, edge):
    sums = jnp.transpose(total)
    return (sums[:edge] / jnp.maximum(sums[edge : edge + 1], 1.0)).astype(BF16)


def prepare_kernel(count, edge, slots, *refs):
    lay_out(refs[:slots], count, edge, refs[-1], *refs[-5:-1])


def render_kernel(count, edge, groups, *refs):
    prepared = refs[: 4 * len(groups)]
    smooth_a, smooth_b, out_ref = refs[4 * len(groups) : 4 * len(groups) + 3]
    stacks = refs[4 * len(groups) + 3 :]
    me = lax.axis_index("strip")
    smooth = smooth_a[...] + smooth_b[...]
    total = None
    for i, offsets in enumerate(groups):
        onehot, base, grad_y, grad_x = prepared[4 * i : 4 * i + 4]
        for slot, offset in enumerate(offsets):
            strip = jnp.bitwise_xor(me, offset)
            align_rows(smooth, strip, count, edge, slot, base, grad_y, grad_x, stacks[i])
        used = len(offsets) * count * edge
        if stacks[i].shape[0] > used:
            stacks[i][used:, :] = base[used:, :]
        part = product(onehot[...], stacks[i][...])
        total = part if total is None else total + part
    out_ref[...] = averaged(total, edge)


def render_all_kernel(
    count, edge, messages, smooth_ref, out_ref, onehot, base, grad_y, grad_x, keys, stacked
):
    rows = count * edge

    def step(i, total):
        lay_out([messages.at[i]], count, edge, keys, onehot, base, grad_y, grad_x)
        align_rows(smooth_ref[...], i, count, edge, 0, base, grad_y, grad_x, stacked)
        if stacked.shape[0] > rows:
            stacked[rows:, :] = base[rows:, :]
        return total + product(onehot[...], stacked[...])

    total = lax.fori_loop(0, messages.shape[0], step, jnp.zeros((rows, 2 * LANES), F32))
    out_ref[...] = averaged(total, edge)


def turned(block, axis, distance):
    size = lax.axis_size(axis)
    return lax.ppermute(block, axis, [(i, (i + distance) % size) for i in range(size)])


def swapped(block, offset):
    return lax.ppermute(
        block, "strip", [(i, i ^ offset) for i in range(lax.axis_size("strip"))]
    )


def on_device(image, peaks, row_source, row_weight, col_source, col_weight, owner, render_row):
    pixels = image[0]
    count, edge, _ = pixels.shape
    rows = count * edge
    sections, strips = lax.axis_size("sec"), lax.axis_size("strip")
    dft_cos, dft_sin = dft_tables(edge)
    length = message_rows(rows)
    wide = round_up(rows, LANES)

    inputs = (
        pixels,
        row_source[0],
        row_weight[0],
        col_source[0],
        col_weight[0],
        owner[0].reshape(1, rows),
        render_row,
    )
    message = call(
        base_kernel,
        jax.ShapeDtypeStruct((length, LANES), BF16),
        len(inputs),
        space=pltpu.HBM,
        scratch=[pltpu.VMEM(x.shape, x.dtype) for x in inputs]
        + [pltpu.VMEM((16, wide), F32), pltpu.SemaphoreType.DMA((len(inputs),))],
    )(*[pltpu.with_memory_space_constraint(x, pltpu.HBM) for x in inputs])
    prior_message = turned(message, "sec", 1)

    def table(*shape, kind=BF16):
        return jax.ShapeDtypeStruct(shape, kind)

    square = table(count, edge, edge, kind=F32)
    slim, tall = table(count, 16, edge), table(count, edge, LANES)
    *spectra, copied = call(
        spectrum_kernel,
        (square, square, slim, slim, tall, tall, table(length, LANES)),
        5,
    )(pixels, dft_cos, dft_sin, peaks[0], message)
    near, cross_re, cross_im = call(
        near_kernel,
        (table(8, LANES, kind=F32), table(count, edge, edge), table(count, edge, edge)),
        9,
    )(prior_message, *spectra[:2], dft_cos, dft_sin, *spectra[2:])

    surfaces = call(surface_kernel, (square,) * 3, 4)(cross_re, cross_im, dft_cos, dft_sin)

    def laid(slots):
        deep = round_up(slots * rows, LANES)
        return (table(rows, deep),) + (table(deep, 2 * LANES),) * 3

    def key_line(slots):
        return pltpu.VMEM((8, round_up(slots * rows, LANES)), F32)

    def stack(slots):
        return pltpu.VMEM((round_up(slots * rows, LANES), 2 * LANES), BF16)

    few = strips <= 8 and strips & (strips - 1) == 0
    order = [surfaces[0]]
    if few:
        offsets = [2 * k for k in range(strips // 2)]
        blocks = [copied] + [swapped(copied, offset) for offset in offsets[1:]]

        def prepared(group, after):
            return call(
                functools.partial(prepare_kernel, count, edge, len(group)),
                laid(len(group)),
                len(group) + 1,
                scratch=[key_line(len(group))],
            )(*group, after)

        early_side = prepared([copied, swapped(message, 1)], near)
        order.append(early_side[0])

    nears = [near] + [turned(near, "sec", k) for k in range(1, sections - 1)]
    patches_all = round_up(count * strips, LANES)
    smooth, prior = call(
        functools.partial(chain_kernel, count, len(nears)),
        (table(8, patches_all, kind=F32), table(8, LANES, kind=F32)),
        len(nears) + len(order),
    )(*nears, *order)
    corr_map, passed = call(map_kernel, (square, table(8, patches_all, kind=F32)), 5)(
        *surfaces, prior, smooth
    )

    rendered = table(edge, rows)
    if few:
        total = sum([swapped(smooth, offset) for offset in offsets[1:]], passed)
        late_side = prepared(blocks[1:] + [swapped(block, 1) for block in blocks[1:]], total)
        groups = [0, 1], offsets[1:] + [offset + 1 for offset in offsets[1:]]
        render = call(
            functools.partial(render_kernel, count, edge, groups),
            rendered,
            10,
            scratch=[stack(len(group)) for group in groups],
        )(*early_side, *late_side, total, swapped(total, 1))
    else:
        render = call(
            functools.partial(render_all_kernel, count, edge),
            rendered,
            2,
            scratch=[pltpu.VMEM(x.shape, x.dtype) for x in laid(1)] + [key_line(1), stack(1)],
            vmem=2 * strips * length * LANES * 2 + VMEM_BYTES,
        )(lax.all_gather(copied, "strip"), lax.psum(passed, "strip"))
    return (render.T[None], corr_map[None])


def solution(mesh):
    placed = (
        P("sec", "strip", None, None),
        P("sec", "strip", None),
        P("sec", "strip", None),
        P("sec", "strip", None),
        P("sec", "strip", None),
        P("sec", "strip", None),
        P("sec", "strip", None),
        P("sec", "strip"),
    )
    return jax.shard_map(
        on_device,
        mesh=mesh,
        in_specs=placed,
        out_specs=(P("sec", "strip", None), P("sec", "strip", None, None)),
        check_vma=False,
    )
```

time: 32.5 us -> 29.3 us (0.902)
  local copies, waits for them, and re-layouts: 3.07 us -> 0.02 us
  waiting for transfers between devices: 7.98 us -> 5.35 us
  Pallas kernels: 6.24 us -> 8.59 us
    unnamed x21 -> x8, local copies, waits for them, and re-layouts: 3.07 us -> 0.02 us
    pallas_call x6 -> x9, Pallas kernels: 6.24 us -> 8.59 us  [the longest x1 1.64 us: on_device(): call(base_kernel, jax.ShapeDtypeStruct((length, LANES), BF16), len(inputs...]
    ppermute x11, waiting for transfers between devices: 4.66 us -> 2.43 us  [swapped(): lax.ppermute(block, 'strip', [(i, i ^ offset) for i in range(lax.axis_siz...]
    ppermute x3, waiting for transfers between devices: 3.32 us -> 2.91 us  [turned(): lax.ppermute(block, axis, [(i, (i + distance) % size) for i in range(size)])]
  transfers between devices with their start and end apart: 14 -> 14, of which waited for: 4 -> 4; matrix products, arithmetic and copies ran while one was open for 0% -> 0% of each run, Pallas kernels for 12% -> 18%
where the time goes in v1:
time: 29.3 us; the launch traced here: 29.2 us
  starting transfers between devices  14.4 us (49%)
  Pallas kernels  8.59 us (29%)
  waiting for transfers between devices  5.35 us (18%)
  between operations  0.78 us (3%)
    ppermute x11, starting transfers between devices, swapped(): lax.ppermute(block, 'strip', [(i, i ^ offset) for i in range(lax.axis_siz...  9.56 us
    ppermute x3, starting transfers between devices, turned(): lax.ppermute(block, axis, [(i, (i + distance) % size) for i in range(size)])  4.87 us
    ppermute x3, waiting for transfers between devices, turned(): lax.ppermute(block, axis, [(i, (i + distance) % size) for i in range(size)])  2.91 us
    ppermute x11, waiting for transfers between devices, swapped(): lax.ppermute(block, 'strip', [(i, i ^ offset) for i in range(lax.axis_siz...  2.43 us
    pallas_call x1, Pallas kernels, on_device(): call(base_kernel, jax.ShapeDtypeStruct((length, LANES), BF16), len(inputs...  1.64 us
    pallas_call x1, Pallas kernels, on_device(): call(functools.partial(render_kernel, count, edge, groups), rendered, 10,...  1.62 us
    pallas_call x2, Pallas kernels, prepared(): call(functools.partial(prepare_kernel, count, edge, len(group)), laid(len...  1.37 us
    pallas_call x1, Pallas kernels, on_device(): call(near_kernel, (table(8, LANES, kind=F32), table(count, edge, edge), t...  1.02 us
  transfers between devices with their start and end apart: 14, of which 4 were waited for; matrix products, arithmetic and copies ran while one was open for 0% of the time, Pallas kernels for 18%

profile of v1, /device:TPU:0, one launch (start us, length us, event | category | flops | bytes accessed | tf_op | source)
XLA Modules:
  0.0 29.2 jit_solution(10736754540756757968)
XLA Ops:
  0.6 0.0 copy-start
  0.6 0.0 copy-start.1
  0.7 0.0 copy-start.2
  0.7 0.0 copy-start.3
  0.7 1.6 %shard_map.113.message_ref = bf16[416,128]{1,0:T(8,128)(2,1)S(1)} custom-call(bf16[2,160,160]{2,1,0:T(8,128)(2,1)} %bitcast.11, s32[2,160]{1,0:T(2,128)} %bitcast.15, f32[2,160]{1,0:T(2,128)} %bitcast.16, s32[2,160]{1,0:T(2,128)} %bitcast.17, f32[2,160]{1,0:T(2,128)} %bitcast.18, s32[1,320]{1,0:T(1,128)} %bitcast.19, s32[1,320]{1,0:T(1,128)} %refs_6_.1), custom_call_target="tpu_custom_call" | custom-call | flops 1000000000 | bytes 500000 | tf_op jit(solution)/shard_map/pallas_call | solution.py:420
  2.3 3.0 %collective-permute-start.1 = (bf16[416,128]{1,0:T(8,128)(2,1)S(1)}, bf16[416,128]{1,0:T(8,128)(2,1)S(1)}, u32[]{:S(2)}, u32[]{:S(2)}) collective-permute-start(bf16[416,128]{1,0:T(8,128)(2,1)S(1)} %shard_map.113.message_ref), channel_id=1, source_target_pairs={{0,8},{8,16},{16,24},{24,0},{1,9},{9,17},{17,25},{25,1},{2,10},{10... | collective-permute-start | bytes 319496 | tf_op jit(solution)/shard_map/ppermute | solution.py:393
  5.3 0.0 collective-permute-start
  5.3 0.0 copy-done
  5.3 0.0 copy-done.1
  5.3 0.0 copy-done.2
  5.3 0.0 copy-done.3
  5.3 0.7 %shard_map.114 = (f32[2,160,160]{2,1,0:T(8,128)S(1)}, f32[2,160,160]{2,1,0:T(8,128)S(1)}, bf16[2,16,160]{2,1,0:T(8,128)(2,1)S(1)}, bf16[2,16,160]{2,1,0:T(8,128)...) custom-call(bf16[2,160,160]{2,1,0:T(8,128)(2,1)S(1)} %bitcast.12, ...), custom_call_target="tpu_custom_call" | custom-call | flops 1000000000 | bytes 500000 | tf_op jit(solution)/shard_map/pallas_call | solution.py:435
  6.0 1.6 %collective-permute-start.2 = (bf16[416,128]{1,0:T(8,128)(2,1)S(1)}, bf16[416,128]{1,0:T(8,128)(2,1)S(1)}, u32[]{:S(2)}, u32[]{:S(2)}) collective-permute-start(bf16[416,128]{1,0:T(8,128)(2,1)S(1)} %get-tuple-element.27.refs_0_), channel_id=1, source_target_pairs={{0,2},{1,3},{2,0},{3,1},{4,6},{5,7},{6,4},{7,5},{8,10},{9,11},{10,... | collective-permute-start | bytes 319496 | tf_op jit(solution)/shard_map/ppermute | solution.py:397
  7.7 2.6 %collective-permute-start.3 = (bf16[416,128]{1,0:T(8,128)(2,1)S(1)}, bf16[416,128]{1,0:T(8,128)(2,1)S(1)}, u32[]{:S(2)}, u32[]{:S(2)}) collective-permute-start(bf16[416,128]{1,0:T(8,128)(2,1)S(1)} %get-tuple-element.27.refs_0_), channel_id=1, source_target_pairs={{0,4},{1,5},{2,6},{3,7},{4,0},{5,1},{6,2},{7,3},{8,12},{9,13},{10,... | collective-permute-start | bytes 319496 | tf_op jit(solution)/shard_map/ppermute | solution.py:397
  10.2 0.2 collective-permute-start.4
  10.5 0.0 collective-permute-done.1.message_ref
  10.5 1.0 %shard_map.115 = (f32[8,128]{1,0:T(8,128)S(1)}, bf16[2,160,160]{2,1,0:T(8,128)(2,1)S(1)}, bf16[2,160,160]{2,1,0:T(8,128)(2,1)S(1)}) custom-call(bf16[416,128]{1,0:T(8,128)(2,1)S(1)} %collective-permute-done.1.message_ref, f32[2,160,160]{2,1,0:T(8,128)S(1)} %get-tuple-element.28.im_re_ref, f32[2,160,160]{2,1,0:T(8,128)S(1)} %get-tuple-element.29.im_im_ref, ...), custom_call_target="tpu_custom_call" | custom-call | flops 1000000000 | bytes 500000 | tf_op jit(solution)/shard_map/pallas_call | solution.py:440
  11.5 1.5 %collective-permute-start.8 = (f32[8,128]{1,0:T(8,128)S(1)}, f32[8,128]{1,0:T(8,128)S(1)}, u32[]{:S(2)}, u32[]{:S(2)}) collective-permute-start(f32[8,128]{1,0:T(8,128)S(1)} %get-tuple-element.34.refs_2_.refs_0_), channel_id=1, source_target_pairs={{0,8},{8,16},{16,24},{24,0},{1,9},{9,17},{17,25},{25,1},{2,10},{10... | collective-permute-start | bytes 12296 | tf_op jit(solution)/shard_map/ppermute | solution.py:393
  13.0 0.8 %shard_map.117 = (f32[2,160,160]{2,1,0:T(8,128)S(1)}, f32[2,160,160]{2,1,0:T(8,128)S(1)}, f32[2,160,160]{2,1,0:T(8,128)S(1)}) custom-call(bf16[2,160,160]{2,1,0:T(8,128)(2,1)S(1)} %get-tuple-element.39.cross_re_ref, bf16[2,160,160]{2,1,0:T(8,128)(2,1)S(1)} %get-tuple-element.40.cross_im_ref, bf16[160,160]{1,0:T(8,128)(2,1)S(1)} %copy-done.2, ...), custom_call_target="tpu_custom_call" | custom-call | flops 1000000000 | bytes 500000 | tf_op jit(solution)/shard_map/pallas_call | solution.py:446
  13.9 0.0 collective-permute-done.refs_1_
  13.9 0.4 %collective-permute-start.9 = (f32[8,128]{1,0:T(8,128)S(1)}, f32[8,128]{1,0:T(8,128)S(1)}, u32[]{:S(2)}, u32[]{:S(2)}) collective-permute-start(f32[8,128]{1,0:T(8,128)S(1)} %get-tuple-element.34.refs_2_.refs_0_), channel_id=1, source_target_pairs={{0,16},{8,24},{16,0},{24,8},{1,17},{9,25},{17,1},{25,9},{2,18},{10... | collective-permute-start | bytes 12296 | tf_op jit(solution)/shard_map/ppermute | solution.py:393
  14.2 0.4 %shard_map.116 = (bf16[320,640]{1,0:T(8,128)(2,1)S(1)}, bf16[640,256]{1,0:T(8,128)(2,1)S(1)}, bf16[640,256]{1,0:T(8,128)(2,1)S(1)}, bf16[640,256]{1,0:T(8,128)(2,1)S(1)}) custom-call(bf16[416,128]{1,0:T(8,128)(2,1)S(1)} %get-tuple-element.27.refs_0_, bf16[416,128]{1,0:T(8,128)(2,1)S(1)} %collective-permute-done.refs_1_, ...), custom_call_target="tpu_custom_call" | custom-call | flops 1000000000 | bytes 500000 | tf_op jit(solution)/shard_map/pallas_call | solution.py:465
  14.6 1.4 %collective-permute-done.8.refs_1_ = f32[8,128]{1,0:T(8,128)S(1)} collective-permute-done((f32[8,128]{1,0:T(8,128)S(1)}, f32[8,128]{1,0:T(8,128)S(1)}, u32[]{:S(2)}, u32[]{:S(2)}) %collective-permute-start.8) | collective-permute-done | bytes 4128 | tf_op jit(solution)/shard_map/ppermute | solution.py:393
  16.1 1.5 %collective-permute-done.9.refs_2_ = f32[8,128]{1,0:T(8,128)S(1)} collective-permute-done((f32[8,128]{1,0:T(8,128)S(1)}, f32[8,128]{1,0:T(8,128)S(1)}, u32[]{:S(2)}, u32[]{:S(2)}) %collective-permute-start.9) | collective-permute-done | bytes 4128 | tf_op jit(solution)/shard_map/ppermute | solution.py:393
  17.6 0.6 %shard_map.118 = (f32[8,128]{1,0:T(8,128)S(1)}, f32[8,128]{1,0:T(8,128)S(1)}) custom-call(f32[8,128]{1,0:T(8,128)S(1)} %get-tuple-element.34.refs_2_.refs_0_, f32[8,128]{1,0:T(8,128)S(1)} %collective-permute-done.8.refs_1_, f32[8,128]{1,0:T(8,128)S(1)} %collective-permute-done.9.refs_2_, f32[2,160,160]{2,1,0:T(8,128)S(1)} %get-tuple-element.41.refs_3_.corr_ref, ...), custom_call_target="tpu_custom_call" | custom-call | flops 1000000000 | bytes 500000 | tf_op jit(solution)/shard_map/pallas_call | solution.py:477
  18.1 3.7 %collective-permute-start.12 = (f32[8,128]{1,0:T(8,128)S(1)}, f32[8,128]{1,0:T(8,128)S(1)}, u32[]{:S(2)}, u32[]{:S(2)}) collective-permute-start(f32[8,128]{1,0:T(8,128)S(1)} %get-tuple-element.45.smooth_ref), channel_id=1, source_target_pairs={{0,6},{1,7},{2,4},{3,5},{4,2},{5,3},{6,0},{7,1},{8,14},{9,15},{10,... | collective-permute-start | bytes 12296 | tf_op jit(solution)/shard_map/ppermute | solution.py:397
  21.8 0.0 collective-permute-start.11
  21.8 0.0 collective-permute-done.2.refs_0_
  21.8 0.8 %collective-permute-start.10 = (f32[8,128]{1,0:T(8,128)S(1)}, f32[8,128]{1,0:T(8,128)S(1)}, u32[]{:S(2)}, u32[]{:S(2)}) collective-permute-start(f32[8,128]{1,0:T(8,128)S(1)} %get-tuple-element.45.smooth_ref), channel_id=1, source_target_pairs={{0,2},{1,3},{2,0},{3,1},{4,6},{5,7},{6,4},{7,5},{8,10},{9,11},{10,... | collective-permute-start | bytes 12296 | tf_op jit(solution)/shard_map/ppermute | solution.py:397
  22.6 0.9 %shard_map.119 = (f32[2,160,160]{2,1,0:T(8,128)}, f32[8,128]{1,0:T(8,128)S(1)}) custom-call(f32[2,160,160]{2,1,0:T(8,128)S(1)} %get-tuple-element.41.refs_3_.corr_ref, f32[2,160,160]{2,1,0:T(8,128)S(1)} %get-tuple-element.42.grad_y_ref, f32[2,160,160]{2,1,0:T(8,128)S(1)} %get-tuple-element.43.grad_x_ref, f32[8,128]{1,0:T(8,128)S(1)} %get-tuple-element.44.prior_ref, ...), custom_call_target="tpu_custom_call" | custom-call | flops 1000000000 | bytes 500000 | tf_op jit(solution)/shard_map/pallas_call | solution.py:482
  23.5 0.0 collective-permute-done.3.refs_1_
  23.5 0.0 collective-permute-start.5
  23.5 0.0 collective-permute-done.4.refs_2_
  23.5 0.5 %collective-permute-start.6 = (bf16[416,128]{1,0:T(8,128)(2,1)S(1)}, bf16[416,128]{1,0:T(8,128)(2,1)S(1)}, u32[]{:S(2)}, u32[]{:S(2)}) collective-permute-start(bf16[416,128]{1,0:T(8,128)(2,1)S(1)} %collective-permute-done.3.refs_1_), channel_id=1, source_target_pairs={{0,1},{1,0},{2,3},{3,2},{4,5},{5,4},{6,7},{7,6},{8,9},{9,8},{10,11... | collective-permute-start | bytes 319496 | tf_op jit(solution)/shard_map/ppermute | solution.py:397
  24.0 0.0 collective-permute-done.12
  24.0 0.1 collective-permute-start.7
  24.0 2.3 %collective-permute-done.11 = f32[8,128]{1,0:T(8,128)S(1)} collective-permute-done((f32[8,128]{1,0:T(8,128)S(1)}, f32[8,128]{1,0:T(8,128)S(1)}, u32[]{:S(2)}, u32[]{:S(2)}) %collective-permute-start.11) | collective-permute-done | bytes 4128 | tf_op jit(solution)/shard_map/ppermute | solution.py:397
  26.3 0.0 collective-permute-done.10
  26.3 0.1 collective-permute-start.13
  26.4 0.0 collective-permute-done.5.refs_3_
  26.4 0.0 collective-permute-done.6.refs_4_
  26.4 0.0 collective-permute-done.7.refs_5_
  26.4 1.0 %shard_map.120 = (bf16[320,1920]{1,0:T(8,128)(2,1)S(1)}, bf16[1920,256]{1,0:T(8,128)(2,1)S(1)}, bf16[1920,256]{1,0:T(8,128)(2,1)S(1)}, bf16[1920,256]{1,0:T(8,128)(2,1)S(1)}) custom-call(bf16[416,128]{1,0:T(8,128)(2,1)S(1)} %collective-permute-done.2.refs_0_, bf16[416,128]{1,0:T(8,128)(2,1)S(1)} %collective-permute-done.3.refs_1_, ...), custom_call_target="tpu_custom_call" | custom-call | flops 1000000000 | bytes 500000 | tf_op jit(solution)/shard_map/pallas_call | solution.py:465
  27.4 0.1 collective-permute-done.13.refs_9_
  27.6 1.6 %shard_map.121 = bf16[160,320]{1,0:T(8,128)(2,1)} custom-call(bf16[320,640]{1,0:T(8,128)(2,1)S(1)} %get-tuple-element.35.refs_4_.refs_0_, bf16[640,256]{1,0:T(8,128)(2,1)S(1)} %get-tuple-element.36.refs_1_, bf16[640,256]{1,0:T(8,128)(2,1)S(1)} %get-tuple-element.37.refs_2_, bf16[640,256]{1,0:T(8,128)(2,1)S(1)} %get-tuple-element.38.refs_3_, ...), custom_call_target="tpu_custom_call" | custom-call | flops 1000000000 | bytes 500000 | tf_op jit(solution)/shard_map/pallas_call | solution.py:491
  (1 shorter events, 0.0 us)
Async XLA Ops:
  0.6 4.7 %copy-start = (bf16[1,2,160,160]{3,2,1,0:T(8,128)(2,1)S(1)}, bf16[1,2,160,160]{3,2,1,0:T(8,128)(2,1)}, u32[]{:S(2)}) copy-start(bf16[1,2,160,160]{3,2,1,0:T(8,128)(2,1)} %param.10) | copy-start | bytes 307204
  0.6 4.7 %copy-start.1 = (s32[1,2,2]{2,1,0:T(2,128)S(1)}, s32[1,2,2]{2,1,0:T(2,128)}, u32[]{:S(2)}) copy-start(s32[1,2,2]{2,1,0:T(2,128)} %param.11) | copy-start | bytes 52
  0.7 4.7 %copy-start.2 = (bf16[160,160]{1,0:T(8,128)(2,1)S(1)}, bf16[160,160]{1,0:T(8,128)(2,1)}, u32[]{:S(2)}) copy-start(bf16[160,160]{1,0:T(8,128)(2,1)} %constant.4.clone.cos_ref) | copy-start | bytes 153604
  0.7 4.7 %copy-start.3 = (bf16[160,160]{1,0:T(8,128)(2,1)S(1)}, bf16[160,160]{1,0:T(8,128)(2,1)}, u32[]{:S(2)}) copy-start(bf16[160,160]{1,0:T(8,128)(2,1)} %constant.5.clone.sin_ref) | copy-start | bytes 153604
  2.3 8.1 %collective-permute-start.1 = (bf16[416,128]{1,0:T(8,128)(2,1)S(1)}, bf16[416,128]{1,0:T(8,128)(2,1)S(1)}, u32[]{:S(2)}, u32[]{:S(2)}) collective-permute-start(bf16[416,128]{1,0:T(8,128)(2,1)S(1)} %shard_map.113.message_ref), channel_id=1, source_target_pairs={{0,8},{8,16},{16,24},{24,0},{1,9},{9,17},{17,25},{25,1},{2,10},{10... | collective-permute-start | bytes 319496 | tf_op jit(solution)/shard_map/ppermute | solution.py:393
  5.3 8.6 %collective-permute-start = (bf16[416,128]{1,0:T(8,128)(2,1)S(1)}, bf16[416,128]{1,0:T(8,128)(2,1)S(1)}, u32[]{:S(2)}, u32[]{:S(2)}) collective-permute-start(bf16[416,128]{1,0:T(8,128)(2,1)S(1)} %shard_map.113.message_ref), channel_id=1, source_target_pairs={{0,1},{1,0},{2,3},{3,2},{4,5},{5,4},{6,7},{7,6},{8,9},{9,8},{10,11... | collective-permute-start | bytes 319496 | tf_op jit(solution)/shard_map/ppermute | solution.py:397
  6.0 15.8 %collective-permute-start.2 = (bf16[416,128]{1,0:T(8,128)(2,1)S(1)}, bf16[416,128]{1,0:T(8,128)(2,1)S(1)}, u32[]{:S(2)}, u32[]{:S(2)}) collective-permute-start(bf16[416,128]{1,0:T(8,128)(2,1)S(1)} %get-tuple-element.27.refs_0_), channel_id=1, source_target_pairs={{0,2},{1,3},{2,0},{3,1},{4,6},{5,7},{6,4},{7,5},{8,10},{9,11},{10,... | collective-permute-start | bytes 319496 | tf_op jit(solution)/shard_map/ppermute | solution.py:397
  7.7 15.8 %collective-permute-start.3 = (bf16[416,128]{1,0:T(8,128)(2,1)S(1)}, bf16[416,128]{1,0:T(8,128)(2,1)S(1)}, u32[]{:S(2)}, u32[]{:S(2)}) collective-permute-start(bf16[416,128]{1,0:T(8,128)(2,1)S(1)} %get-tuple-element.27.refs_0_), channel_id=1, source_target_pairs={{0,4},{1,5},{2,6},{3,7},{4,0},{5,1},{6,2},{7,3},{8,12},{9,13},{10,... | collective-permute-start | bytes 319496 | tf_op jit(solution)/shard_map/ppermute | solution.py:397
  10.2 13.2 %collective-permute-start.4 = (bf16[416,128]{1,0:T(8,128)(2,1)S(1)}, bf16[416,128]{1,0:T(8,128)(2,1)S(1)}, u32[]{:S(2)}, u32[]{:S(2)}) collective-permute-start(bf16[416,128]{1,0:T(8,128)(2,1)S(1)} %get-tuple-element.27.refs_0_), channel_id=1, source_target_pairs={{0,6},{1,7},{2,4},{3,5},{4,2},{5,3},{6,0},{7,1},{8,14},{9,15},{10,... | collective-permute-start | bytes 319496 | tf_op jit(solution)/shard_map/ppermute | solution.py:397
  11.5 4.6 %collective-permute-start.8 = (f32[8,128]{1,0:T(8,128)S(1)}, f32[8,128]{1,0:T(8,128)S(1)}, u32[]{:S(2)}, u32[]{:S(2)}) collective-permute-start(f32[8,128]{1,0:T(8,128)S(1)} %get-tuple-element.34.refs_2_.refs_0_), channel_id=1, source_target_pairs={{0,8},{8,16},{16,24},{24,0},{1,9},{9,17},{17,25},{25,1},{2,10},{10... | collective-permute-start | bytes 12296 | tf_op jit(solution)/shard_map/ppermute | solution.py:393
  13.9 3.7 %collective-permute-start.9 = (f32[8,128]{1,0:T(8,128)S(1)}, f32[8,128]{1,0:T(8,128)S(1)}, u32[]{:S(2)}, u32[]{:S(2)}) collective-permute-start(f32[8,128]{1,0:T(8,128)S(1)} %get-tuple-element.34.refs_2_.refs_0_), channel_id=1, source_target_pairs={{0,16},{8,24},{16,0},{24,8},{1,17},{9,25},{17,1},{25,9},{2,18},{10... | collective-permute-start | bytes 12296 | tf_op jit(solution)/shard_map/ppermute | solution.py:393
  18.1 5.8 %collective-permute-start.12 = (f32[8,128]{1,0:T(8,128)S(1)}, f32[8,128]{1,0:T(8,128)S(1)}, u32[]{:S(2)}, u32[]{:S(2)}) collective-permute-start(f32[8,128]{1,0:T(8,128)S(1)} %get-tuple-element.45.smooth_ref), channel_id=1, source_target_pairs={{0,6},{1,7},{2,4},{3,5},{4,2},{5,3},{6,0},{7,1},{8,14},{9,15},{10,... | collective-permute-start | bytes 12296 | tf_op jit(solution)/shard_map/ppermute | solution.py:397
  21.8 4.5 %collective-permute-start.11 = (f32[8,128]{1,0:T(8,128)S(1)}, f32[8,128]{1,0:T(8,128)S(1)}, u32[]{:S(2)}, u32[]{:S(2)}) collective-permute-start(f32[8,128]{1,0:T(8,128)S(1)} %get-tuple-element.45.smooth_ref), channel_id=1, source_target_pairs={{0,4},{1,5},{2,6},{3,7},{4,0},{5,1},{6,2},{7,3},{8,12},{9,13},{10,... | collective-permute-start | bytes 12296 | tf_op jit(solution)/shard_map/ppermute | solution.py:397
  21.8 4.5 %collective-permute-start.10 = (f32[8,128]{1,0:T(8,128)S(1)}, f32[8,128]{1,0:T(8,128)S(1)}, u32[]{:S(2)}, u32[]{:S(2)}) collective-permute-start(f32[8,128]{1,0:T(8,128)S(1)} %get-tuple-element.45.smooth_ref), channel_id=1, source_target_pairs={{0,2},{1,3},{2,0},{3,1},{4,6},{5,7},{6,4},{7,5},{8,10},{9,11},{10,... | collective-permute-start | bytes 12296 | tf_op jit(solution)/shard_map/ppermute | solution.py:397
  23.5 2.9 %collective-permute-start.5 = (bf16[416,128]{1,0:T(8,128)(2,1)S(1)}, bf16[416,128]{1,0:T(8,128)(2,1)S(1)}, u32[]{:S(2)}, u32[]{:S(2)}) collective-permute-start(bf16[416,128]{1,0:T(8,128)(2,1)S(1)} %collective-permute-done.2.refs_0_), channel_id=1, source_target_pairs={{0,1},{1,0},{2,3},{3,2},{4,5},{5,4},{6,7},{7,6},{8,9},{9,8},{10,11... | collective-permute-start | bytes 319496 | tf_op jit(solution)/shard_map/ppermute | solution.py:397
  23.5 2.9 %collective-permute-start.6 = (bf16[416,128]{1,0:T(8,128)(2,1)S(1)}, bf16[416,128]{1,0:T(8,128)(2,1)S(1)}, u32[]{:S(2)}, u32[]{:S(2)}) collective-permute-start(bf16[416,128]{1,0:T(8,128)(2,1)S(1)} %collective-permute-done.3.refs_1_), channel_id=1, source_target_pairs={{0,1},{1,0},{2,3},{3,2},{4,5},{5,4},{6,7},{7,6},{8,9},{9,8},{10,11... | collective-permute-start | bytes 319496 | tf_op jit(solution)/shard_map/ppermute | solution.py:397
  24.0 2.5 %collective-permute-start.7 = (bf16[416,128]{1,0:T(8,128)(2,1)S(1)}, bf16[416,128]{1,0:T(8,128)(2,1)S(1)}, u32[]{:S(2)}, u32[]{:S(2)}) collective-permute-start(bf16[416,128]{1,0:T(8,128)(2,1)S(1)} %collective-permute-done.4.refs_2_), channel_id=1, source_target_pairs={{0,1},{1,0},{2,3},{3,2},{4,5},{5,4},{6,7},{7,6},{8,9},{9,8},{10,11... | collective-permute-start | bytes 319496 | tf_op jit(solution)/shard_map/ppermute | solution.py:397
  26.3 1.2 %collective-permute-start.13 = (f32[8,128]{1,0:T(8,128)S(1)}, f32[8,128]{1,0:T(8,128)S(1)}, u32[]{:S(2)}, u32[]{:S(2)}) collective-permute-start(f32[8,128]{1,0:T(8,128)S(1)} %add_add_fusion.refs_6_.refs_8_), channel_id=1, source_target_pairs={{0,1},{1,0},{2,3},{3,2},{4,5},{5,4},{6,7},{7,6},{8,9},{9,8},{10,11... | collective-permute-start | bytes 12296 | tf_op jit(solution)/shard_map/ppermute | solution.py:397

commit v2 on v1

--- a/solution.py
+++ b/solution.py
@@ -459,7 +459,10 @@
     order = [surfaces[0]]
     if few:
         offsets = [2 * k for k in range(strips // 2)]
-        blocks = [copied] + [swapped(copied, offset) for offset in offsets[1:]]
+        blocks = [copied]
+        for offset in offsets[1:]:
+            far = 1 << offset.bit_length() - 1
+            blocks.append(swapped(copied, far) if offset == far else swapped(blocks[far // 2], offset - far))
 
         def prepared(group, after):
             return call(

time: 29.3 us -> 26.9 us (0.918)
  waiting for transfers between devices: 5.35 us -> 2.61 us
  starting transfers between devices: 14.4 us -> 14.8 us
    ppermute x3, waiting for transfers between devices: 2.91 us -> 0.01 us  [turned(): lax.ppermute(block, axis, [(i, (i + distance) % size) for i in range(size)])]
  transfers between devices with their start and end apart: 14 -> 14, of which waited for: 4 -> 4; matrix products, arithmetic and copies ran while one was open for 0% -> 0% of each run, Pallas kernels for 18% -> 20%
where the time goes in v2:
time: 26.9 us; the launch traced here: 26.8 us
  starting transfers between devices  14.8 us (55%)
  Pallas kernels  8.61 us (32%)
  waiting for transfers between devices  2.61 us (10%)
  between operations  0.78 us (3%)
    ppermute x11, starting transfers between devices, swapped(): lax.ppermute(block, 'strip', [(i, i ^ offset) for i in range(lax.axis_siz...  9.74 us
    ppermute x3, starting transfers between devices, turned(): lax.ppermute(block, axis, [(i, (i + distance) % size) for i in range(size)])  5.03 us
    ppermute x11, waiting for transfers between devices, swapped(): lax.ppermute(block, 'strip', [(i, i ^ offset) for i in range(lax.axis_siz...  2.6 us
    pallas_call x1, Pallas kernels, on_device(): call(functools.partial(render_kernel, count, edge, groups), rendered, 10,...  1.64 us
    pallas_call x1, Pallas kernels, on_device(): call(base_kernel, jax.ShapeDtypeStruct((length, LANES), BF16), len(inputs...  1.64 us
    pallas_call x2, Pallas kernels, prepared(): call(functools.partial(prepare_kernel, count, edge, len(group)), laid(len...  1.37 us
    pallas_call x1, Pallas kernels, on_device(): call(near_kernel, (table(8, LANES, kind=F32), table(count, edge, edge), t...  1.02 us
    pallas_call x1, Pallas kernels, on_device(): call(map_kernel, (square, table(8, patches_all, kind=F32)), 5)  0.86 us
  transfers between devices with their start and end apart: 14, of which 4 were waited for; matrix products, arithmetic and copies ran while one was open for 0% of the time, Pallas kernels for 20%

profile of v2, /device:TPU:0, one launch (start us, length us, event | category | flops | bytes accessed | tf_op | source)
XLA Modules:
  0.0 26.8 jit_solution(14255623054341918261)
XLA Ops:
  0.6 0.0 copy-start
  0.6 0.0 copy-start.1
  0.7 0.0 copy-start.2
  0.7 0.0 copy-start.3
  0.7 1.6 %shard_map.113.message_ref = bf16[416,128]{1,0:T(8,128)(2,1)S(1)} custom-call(bf16[2,160,160]{2,1,0:T(8,128)(2,1)} %bitcast.11, s32[2,160]{1,0:T(2,128)} %bitcast.15, f32[2,160]{1,0:T(2,128)} %bitcast.16, s32[2,160]{1,0:T(2,128)} %bitcast.17, f32[2,160]{1,0:T(2,128)} %bitcast.18, s32[1,320]{1,0:T(1,128)} %bitcast.19, s32[1,320]{1,0:T(1,128)} %refs_6_.1), custom_call_target="tpu_custom_call" | custom-call | flops 1000000000 | bytes 500000 | tf_op jit(solution)/shard_map/pallas_call | solution.py:420
  2.3 3.0 %collective-permute-start.1 = (bf16[416,128]{1,0:T(8,128)(2,1)S(1)}, bf16[416,128]{1,0:T(8,128)(2,1)S(1)}, u32[]{:S(2)}, u32[]{:S(2)}) collective-permute-start(bf16[416,128]{1,0:T(8,128)(2,1)S(1)} %shard_map.113.message_ref), channel_id=1, source_target_pairs={{0,8},{8,16},{16,24},{24,0},{1,9},{9,17},{17,25},{25,1},{2,10},{10... | collective-permute-start | bytes 319496 | tf_op jit(solution)/shard_map/ppermute | solution.py:393
  5.3 0.0 collective-permute-start
  5.3 0.0 copy-done
  5.3 0.0 copy-done.1
  5.3 0.0 copy-done.2
  5.3 0.0 copy-done.3
  5.3 0.7 %shard_map.114 = (f32[2,160,160]{2,1,0:T(8,128)S(1)}, f32[2,160,160]{2,1,0:T(8,128)S(1)}, bf16[2,16,160]{2,1,0:T(8,128)(2,1)S(1)}, bf16[2,16,160]{2,1,0:T(8,128)...) custom-call(bf16[2,160,160]{2,1,0:T(8,128)(2,1)S(1)} %bitcast.12, ...), custom_call_target="tpu_custom_call" | custom-call | flops 1000000000 | bytes 500000 | tf_op jit(solution)/shard_map/pallas_call | solution.py:435
  6.0 1.6 %collective-permute-start.2 = (bf16[416,128]{1,0:T(8,128)(2,1)S(1)}, bf16[416,128]{1,0:T(8,128)(2,1)S(1)}, u32[]{:S(2)}, u32[]{:S(2)}) collective-permute-start(bf16[416,128]{1,0:T(8,128)(2,1)S(1)} %get-tuple-element.27.refs_0_), channel_id=1, source_target_pairs={{0,2},{1,3},{2,0},{3,1},{4,6},{5,7},{6,4},{7,5},{8,10},{9,11},{10,... | collective-permute-start | bytes 319496 | tf_op jit(solution)/shard_map/ppermute | solution.py:397
  7.7 2.6 %collective-permute-start.3 = (bf16[416,128]{1,0:T(8,128)(2,1)S(1)}, bf16[416,128]{1,0:T(8,128)(2,1)S(1)}, u32[]{:S(2)}, u32[]{:S(2)}) collective-permute-start(bf16[416,128]{1,0:T(8,128)(2,1)S(1)} %get-tuple-element.27.refs_0_), channel_id=1, source_target_pairs={{0,4},{1,5},{2,6},{3,7},{4,0},{5,1},{6,2},{7,3},{8,12},{9,13},{10,... | collective-permute-start | bytes 319496 | tf_op jit(solution)/shard_map/ppermute | solution.py:397
  10.2 0.0 collective-permute-done.1.message_ref
  10.2 1.0 %shard_map.115 = (f32[8,128]{1,0:T(8,128)S(1)}, bf16[2,160,160]{2,1,0:T(8,128)(2,1)S(1)}, bf16[2,160,160]{2,1,0:T(8,128)(2,1)S(1)}) custom-call(bf16[416,128]{1,0:T(8,128)(2,1)S(1)} %collective-permute-done.1.message_ref, f32[2,160,160]{2,1,0:T(8,128)S(1)} %get-tuple-element.28.im_re_ref, f32[2,160,160]{2,1,0:T(8,128)S(1)} %get-tuple-element.29.im_im_ref, ...), custom_call_target="tpu_custom_call" | custom-call | flops 1000000000 | bytes 500000 | tf_op jit(solution)/shard_map/pallas_call | solution.py:440
  11.3 1.5 %collective-permute-start.8 = (f32[8,128]{1,0:T(8,128)S(1)}, f32[8,128]{1,0:T(8,128)S(1)}, u32[]{:S(2)}, u32[]{:S(2)}) collective-permute-start(f32[8,128]{1,0:T(8,128)S(1)} %get-tuple-element.34.refs_2_.refs_0_), channel_id=1, source_target_pairs={{0,8},{8,16},{16,24},{24,0},{1,9},{9,17},{17,25},{25,1},{2,10},{10... | collective-permute-start | bytes 12296 | tf_op jit(solution)/shard_map/ppermute | solution.py:393
  12.8 0.5 %collective-permute-start.9 = (f32[8,128]{1,0:T(8,128)S(1)}, f32[8,128]{1,0:T(8,128)S(1)}, u32[]{:S(2)}, u32[]{:S(2)}) collective-permute-start(f32[8,128]{1,0:T(8,128)S(1)} %get-tuple-element.34.refs_2_.refs_0_), channel_id=1, source_target_pairs={{0,16},{8,24},{16,0},{24,8},{1,17},{9,25},{17,1},{25,9},{2,18},{10... | collective-permute-start | bytes 12296 | tf_op jit(solution)/shard_map/ppermute | solution.py:393
  13.3 0.8 %shard_map.117 = (f32[2,160,160]{2,1,0:T(8,128)S(1)}, f32[2,160,160]{2,1,0:T(8,128)S(1)}, f32[2,160,160]{2,1,0:T(8,128)S(1)}) custom-call(bf16[2,160,160]{2,1,0:T(8,128)(2,1)S(1)} %get-tuple-element.39.cross_re_ref, bf16[2,160,160]{2,1,0:T(8,128)(2,1)S(1)} %get-tuple-element.40.cross_im_ref, bf16[160,160]{1,0:T(8,128)(2,1)S(1)} %copy-done.2, ...), custom_call_target="tpu_custom_call" | custom-call | flops 1000000000 | bytes 500000 | tf_op jit(solution)/shard_map/pallas_call | solution.py:446
  14.2 0.0 collective-permute-done.refs_1_
  14.2 0.4 %shard_map.116 = (bf16[320,640]{1,0:T(8,128)(2,1)S(1)}, bf16[640,256]{1,0:T(8,128)(2,1)S(1)}, bf16[640,256]{1,0:T(8,128)(2,1)S(1)}, bf16[640,256]{1,0:T(8,128)(2,1)S(1)}) custom-call(bf16[416,128]{1,0:T(8,128)(2,1)S(1)} %get-tuple-element.27.refs_0_, bf16[416,128]{1,0:T(8,128)(2,1)S(1)} %collective-permute-done.refs_1_, ...), custom_call_target="tpu_custom_call" | custom-call | flops 1000000000 | bytes 500000 | tf_op jit(solution)/shard_map/pallas_call | solution.py:468
  14.6 1.4 %collective-permute-done.3.refs_1_ = bf16[416,128]{1,0:T(8,128)(2,1)S(1)} collective-permute-done((bf16[416,128]{1,0:T(8,128)(2,1)S(1)}, bf16[416,128]{1,0:T(8,128)(2,1)S(1)}, u32[]{:S(2)}, u32[]{:S(2)}) %collective-permute-start.3) | collective-permute-done | bytes 106528 | tf_op jit(solution)/shard_map/ppermute | solution.py:397
  16.0 0.5 %collective-permute-start.4 = (bf16[416,128]{1,0:T(8,128)(2,1)S(1)}, bf16[416,128]{1,0:T(8,128)(2,1)S(1)}, u32[]{:S(2)}, u32[]{:S(2)}) collective-permute-start(bf16[416,128]{1,0:T(8,128)(2,1)S(1)} %collective-permute-done.3.refs_1_), channel_id=1, source_target_pairs={{0,2},{1,3},{2,0},{3,1},{4,6},{5,7},{6,4},{7,5},{8,10},{9,11},{10,... | collective-permute-start | bytes 319496 | tf_op jit(solution)/shard_map/ppermute | solution.py:397
  16.4 0.0 collective-permute-done.8.refs_1_
  16.4 0.0 collective-permute-done.9.refs_2_
  16.4 0.6 %shard_map.118 = (f32[8,128]{1,0:T(8,128)S(1)}, f32[8,128]{1,0:T(8,128)S(1)}) custom-call(f32[8,128]{1,0:T(8,128)S(1)} %get-tuple-element.34.refs_2_.refs_0_, f32[8,128]{1,0:T(8,128)S(1)} %collective-permute-done.8.refs_1_, f32[8,128]{1,0:T(8,128)S(1)} %collective-permute-done.9.refs_2_, f32[2,160,160]{2,1,0:T(8,128)S(1)} %get-tuple-element.41.refs_3_.corr_ref, ...), custom_call_target="tpu_custom_call" | custom-call | flops 1000000000 | bytes 500000 | tf_op jit(solution)/shard_map/pallas_call | solution.py:480
  17.0 2.2 %collective-permute-start.12 = (f32[8,128]{1,0:T(8,128)S(1)}, f32[8,128]{1,0:T(8,128)S(1)}, u32[]{:S(2)}, u32[]{:S(2)}) collective-permute-start(f32[8,128]{1,0:T(8,128)S(1)} %get-tuple-element.45.smooth_ref), channel_id=1, source_target_pairs={{0,6},{1,7},{2,4},{3,5},{4,2},{5,3},{6,0},{7,1},{8,14},{9,15},{10,... | collective-permute-start | bytes 12296 | tf_op jit(solution)/shard_map/ppermute | solution.py:397
  19.2 0.9 %collective-permute-start.11 = (f32[8,128]{1,0:T(8,128)S(1)}, f32[8,128]{1,0:T(8,128)S(1)}, u32[]{:S(2)}, u32[]{:S(2)}) collective-permute-start(f32[8,128]{1,0:T(8,128)S(1)} %get-tuple-element.45.smooth_ref), channel_id=1, source_target_pairs={{0,4},{1,5},{2,6},{3,7},{4,0},{5,1},{6,2},{7,3},{8,12},{9,13},{10,... | collective-permute-start | bytes 12296 | tf_op jit(solution)/shard_map/ppermute | solution.py:397
  20.1 1.4 %collective-permute-start.10 = (f32[8,128]{1,0:T(8,128)S(1)}, f32[8,128]{1,0:T(8,128)S(1)}, u32[]{:S(2)}, u32[]{:S(2)}) collective-permute-start(f32[8,128]{1,0:T(8,128)S(1)} %get-tuple-element.45.smooth_ref), channel_id=1, source_target_pairs={{0,2},{1,3},{2,0},{3,1},{4,6},{5,7},{6,4},{7,5},{8,10},{9,11},{10,... | collective-permute-start | bytes 12296 | tf_op jit(solution)/shard_map/ppermute | solution.py:397
  21.5 0.9 %shard_map.119 = (f32[2,160,160]{2,1,0:T(8,128)}, f32[8,128]{1,0:T(8,128)S(1)}) custom-call(f32[2,160,160]{2,1,0:T(8,128)S(1)} %get-tuple-element.41.refs_3_.corr_ref, f32[2,160,160]{2,1,0:T(8,128)S(1)} %get-tuple-element.42.grad_y_ref, f32[2,160,160]{2,1,0:T(8,128)S(1)} %get-tuple-element.43.grad_x_ref, f32[8,128]{1,0:T(8,128)S(1)} %get-tuple-element.44.prior_ref, ...), custom_call_target="tpu_custom_call" | custom-call | flops 1000000000 | bytes 500000 | tf_op jit(solution)/shard_map/pallas_call | solution.py:485
  22.3 0.0 collective-permute-done.2.refs_0_
  22.3 0.0 collective-permute-start.6
  22.3 0.1 collective-permute-done.12
  22.5 0.4 %collective-permute-start.5 = (bf16[416,128]{1,0:T(8,128)(2,1)S(1)}, bf16[416,128]{1,0:T(8,128)(2,1)S(1)}, u32[]{:S(2)}, u32[]{:S(2)}) collective-permute-start(bf16[416,128]{1,0:T(8,128)(2,1)S(1)} %collective-permute-done.2.refs_0_), channel_id=1, source_target_pairs={{0,1},{1,0},{2,3},{3,2},{4,5},{5,4},{6,7},{7,6},{8,9},{9,8},{10,11... | collective-permute-start | bytes 319496 | tf_op jit(solution)/shard_map/ppermute | solution.py:397
  22.8 0.0 collective-permute-done.4.refs_2_
  22.8 0.1 collective-permute-start.7
  23.0 0.8 %collective-permute-done.11 = f32[8,128]{1,0:T(8,128)S(1)} collective-permute-done((f32[8,128]{1,0:T(8,128)S(1)}, f32[8,128]{1,0:T(8,128)S(1)}, u32[]{:S(2)}, u32[]{:S(2)}) %collective-permute-start.11) | collective-permute-done | bytes 4128 | tf_op jit(solution)/shard_map/ppermute | solution.py:397
  23.8 0.0 collective-permute-done.10
  23.8 0.1 collective-permute-start.13
  23.8 0.0 collective-permute-done.5.refs_3_
  23.9 0.0 collective-permute-done.6.refs_4_
  23.9 0.3 %collective-permute-done.7.refs_5_ = bf16[416,128]{1,0:T(8,128)(2,1)S(1)} collective-permute-done((bf16[416,128]{1,0:T(8,128)(2,1)S(1)}, bf16[416,128]{1,0:T(8,128)(2,1)S(1)}, u32[]{:S(2)}, u32[]{:S(2)}) %collective-permute-start.7) | collective-permute-done | bytes 106528 | tf_op jit(solution)/shard_map/ppermute | solution.py:397
  24.2 1.0 %shard_map.120 = (bf16[320,1920]{1,0:T(8,128)(2,1)S(1)}, bf16[1920,256]{1,0:T(8,128)(2,1)S(1)}, bf16[1920,256]{1,0:T(8,128)(2,1)S(1)}, bf16[1920,256]{1,0:T(8,128)(2,1)S(1)}) custom-call(bf16[416,128]{1,0:T(8,128)(2,1)S(1)} %collective-permute-done.2.refs_0_, bf16[416,128]{1,0:T(8,128)(2,1)S(1)} %collective-permute-done.3.refs_1_, ...), custom_call_target="tpu_custom_call" | custom-call | flops 1000000000 | bytes 500000 | tf_op jit(solution)/shard_map/pallas_call | solution.py:468
  25.1 0.0 collective-permute-done.13.refs_9_
  25.1 1.6 %shard_map.121 = bf16[160,320]{1,0:T(8,128)(2,1)} custom-call(bf16[320,640]{1,0:T(8,128)(2,1)S(1)} %get-tuple-element.35.refs_4_.refs_0_, bf16[640,256]{1,0:T(8,128)(2,1)S(1)} %get-tuple-element.36.refs_1_, bf16[640,256]{1,0:T(8,128)(2,1)S(1)} %get-tuple-element.37.refs_2_, bf16[640,256]{1,0:T(8,128)(2,1)S(1)} %get-tuple-element.38.refs_3_, ...), custom_call_target="tpu_custom_call" | custom-call | flops 1000000000 | bytes 500000 | tf_op jit(solution)/shard_map/pallas_call | solution.py:494
  (1 shorter events, 0.0 us)
Async XLA Ops:
  0.6 4.7 %copy-start = (bf16[1,2,160,160]{3,2,1,0:T(8,128)(2,1)S(1)}, bf16[1,2,160,160]{3,2,1,0:T(8,128)(2,1)}, u32[]{:S(2)}) copy-start(bf16[1,2,160,160]{3,2,1,0:T(8,128)(2,1)} %param.10) | copy-start | bytes 307204
  0.6 4.7 %copy-start.1 = (s32[1,2,2]{2,1,0:T(2,128)S(1)}, s32[1,2,2]{2,1,0:T(2,128)}, u32[]{:S(2)}) copy-start(s32[1,2,2]{2,1,0:T(2,128)} %param.11) | copy-start | bytes 52
  0.7 4.7 %copy-start.2 = (bf16[160,160]{1,0:T(8,128)(2,1)S(1)}, bf16[160,160]{1,0:T(8,128)(2,1)}, u32[]{:S(2)}) copy-start(bf16[160,160]{1,0:T(8,128)(2,1)} %constant.4.clone.cos_ref) | copy-start | bytes 153604
  0.7 4.7 %copy-start.3 = (bf16[160,160]{1,0:T(8,128)(2,1)S(1)}, bf16[160,160]{1,0:T(8,128)(2,1)}, u32[]{:S(2)}) copy-start(bf16[160,160]{1,0:T(8,128)(2,1)} %constant.5.clone.sin_ref) | copy-start | bytes 153604
  2.3 7.9 %collective-permute-start.1 = (bf16[416,128]{1,0:T(8,128)(2,1)S(1)}, bf16[416,128]{1,0:T(8,128)(2,1)S(1)}, u32[]{:S(2)}, u32[]{:S(2)}) collective-permute-start(bf16[416,128]{1,0:T(8,128)(2,1)S(1)} %shard_map.113.message_ref), channel_id=1, source_target_pairs={{0,8},{8,16},{16,24},{24,0},{1,9},{9,17},{17,25},{25,1},{2,10},{10... | collective-permute-start | bytes 319496 | tf_op jit(solution)/shard_map/ppermute | solution.py:393
  5.3 8.8 %collective-permute-start = (bf16[416,128]{1,0:T(8,128)(2,1)S(1)}, bf16[416,128]{1,0:T(8,128)(2,1)S(1)}, u32[]{:S(2)}, u32[]{:S(2)}) collective-permute-start(bf16[416,128]{1,0:T(8,128)(2,1)S(1)} %shard_map.113.message_ref), channel_id=1, source_target_pairs={{0,1},{1,0},{2,3},{3,2},{4,5},{5,4},{6,7},{7,6},{8,9},{9,8},{10,11... | collective-permute-start | bytes 319496 | tf_op jit(solution)/shard_map/ppermute | solution.py:397
  6.0 16.3 %collective-permute-start.2 = (bf16[416,128]{1,0:T(8,128)(2,1)S(1)}, bf16[416,128]{1,0:T(8,128)(2,1)S(1)}, u32[]{:S(2)}, u32[]{:S(2)}) collective-permute-start(bf16[416,128]{1,0:T(8,128)(2,1)S(1)} %get-tuple-element.27.refs_0_), channel_id=1, source_target_pairs={{0,2},{1,3},{2,0},{3,1},{4,6},{5,7},{6,4},{7,5},{8,10},{9,11},{10,... | collective-permute-start | bytes 319496 | tf_op jit(solution)/shard_map/ppermute | solution.py:397
  7.7 8.3 %collective-permute-start.3 = (bf16[416,128]{1,0:T(8,128)(2,1)S(1)}, bf16[416,128]{1,0:T(8,128)(2,1)S(1)}, u32[]{:S(2)}, u32[]{:S(2)}) collective-permute-start(bf16[416,128]{1,0:T(8,128)(2,1)S(1)} %get-tuple-element.27.refs_0_), channel_id=1, source_target_pairs={{0,4},{1,5},{2,6},{3,7},{4,0},{5,1},{6,2},{7,3},{8,12},{9,13},{10,... | collective-permute-start | bytes 319496 | tf_op jit(solution)/shard_map/ppermute | solution.py:397
  11.3 5.2 %collective-permute-start.8 = (f32[8,128]{1,0:T(8,128)S(1)}, f32[8,128]{1,0:T(8,128)S(1)}, u32[]{:S(2)}, u32[]{:S(2)}) collective-permute-start(f32[8,128]{1,0:T(8,128)S(1)} %get-tuple-element.34.refs_2_.refs_0_), channel_id=1, source_target_pairs={{0,8},{8,16},{16,24},{24,0},{1,9},{9,17},{17,25},{25,1},{2,10},{10... | collective-permute-start | bytes 12296 | tf_op jit(solution)/shard_map/ppermute | solution.py:393
  12.8 3.6 %collective-permute-start.9 = (f32[8,128]{1,0:T(8,128)S(1)}, f32[8,128]{1,0:T(8,128)S(1)}, u32[]{:S(2)}, u32[]{:S(2)}) collective-permute-start(f32[8,128]{1,0:T(8,128)S(1)} %get-tuple-element.34.refs_2_.refs_0_), channel_id=1, source_target_pairs={{0,16},{8,24},{16,0},{24,8},{1,17},{9,25},{17,1},{25,9},{2,18},{10... | collective-permute-start | bytes 12296 | tf_op jit(solution)/shard_map/ppermute | solution.py:393
  16.0 6.9 %collective-permute-start.4 = (bf16[416,128]{1,0:T(8,128)(2,1)S(1)}, bf16[416,128]{1,0:T(8,128)(2,1)S(1)}, u32[]{:S(2)}, u32[]{:S(2)}) collective-permute-start(bf16[416,128]{1,0:T(8,128)(2,1)S(1)} %collective-permute-done.3.refs_1_), channel_id=1, source_target_pairs={{0,2},{1,3},{2,0},{3,1},{4,6},{5,7},{6,4},{7,5},{8,10},{9,11},{10,... | collective-permute-start | bytes 319496 | tf_op jit(solution)/shard_map/ppermute | solution.py:397
  17.0 5.5 %collective-permute-start.12 = (f32[8,128]{1,0:T(8,128)S(1)}, f32[8,128]{1,0:T(8,128)S(1)}, u32[]{:S(2)}, u32[]{:S(2)}) collective-permute-start(f32[8,128]{1,0:T(8,128)S(1)} %get-tuple-element.45.smooth_ref), channel_id=1, source_target_pairs={{0,6},{1,7},{2,4},{3,5},{4,2},{5,3},{6,0},{7,1},{8,14},{9,15},{10,... | collective-permute-start | bytes 12296 | tf_op jit(solution)/shard_map/ppermute | solution.py:397
  19.2 4.5 %collective-permute-start.11 = (f32[8,128]{1,0:T(8,128)S(1)}, f32[8,128]{1,0:T(8,128)S(1)}, u32[]{:S(2)}, u32[]{:S(2)}) collective-permute-start(f32[8,128]{1,0:T(8,128)S(1)} %get-tuple-element.45.smooth_ref), channel_id=1, source_target_pairs={{0,4},{1,5},{2,6},{3,7},{4,0},{5,1},{6,2},{7,3},{8,12},{9,13},{10,... | collective-permute-start | bytes 12296 | tf_op jit(solution)/shard_map/ppermute | solution.py:397
  20.1 3.7 %collective-permute-start.10 = (f32[8,128]{1,0:T(8,128)S(1)}, f32[8,128]{1,0:T(8,128)S(1)}, u32[]{:S(2)}, u32[]{:S(2)}) collective-permute-start(f32[8,128]{1,0:T(8,128)S(1)} %get-tuple-element.45.smooth_ref), channel_id=1, source_target_pairs={{0,2},{1,3},{2,0},{3,1},{4,6},{5,7},{6,4},{7,5},{8,10},{9,11},{10,... | collective-permute-start | bytes 12296 | tf_op jit(solution)/shard_map/ppermute | solution.py:397
  22.3 1.5 %collective-permute-start.6 = (bf16[416,128]{1,0:T(8,128)(2,1)S(1)}, bf16[416,128]{1,0:T(8,128)(2,1)S(1)}, u32[]{:S(2)}, u32[]{:S(2)}) collective-permute-start(bf16[416,128]{1,0:T(8,128)(2,1)S(1)} %collective-permute-done.3.refs_1_), channel_id=1, source_target_pairs={{0,1},{1,0},{2,3},{3,2},{4,5},{5,4},{6,7},{7,6},{8,9},{9,8},{10,11... | collective-permute-start | bytes 319496 | tf_op jit(solution)/shard_map/ppermute | solution.py:397
  22.5 1.4 %collective-permute-start.5 = (bf16[416,128]{1,0:T(8,128)(2,1)S(1)}, bf16[416,128]{1,0:T(8,128)(2,1)S(1)}, u32[]{:S(2)}, u32[]{:S(2)}) collective-permute-start(bf16[416,128]{1,0:T(8,128)(2,1)S(1)} %collective-permute-done.2.refs_0_), channel_id=1, source_target_pairs={{0,1},{1,0},{2,3},{3,2},{4,5},{5,4},{6,7},{7,6},{8,9},{9,8},{10,11... | collective-permute-start | bytes 319496 | tf_op jit(solution)/shard_map/ppermute | solution.py:397
  22.8 1.3 %collective-permute-start.7 = (bf16[416,128]{1,0:T(8,128)(2,1)S(1)}, bf16[416,128]{1,0:T(8,128)(2,1)S(1)}, u32[]{:S(2)}, u32[]{:S(2)}) collective-permute-start(bf16[416,128]{1,0:T(8,128)(2,1)S(1)} %collective-permute-done.4.refs_2_), channel_id=1, source_target_pairs={{0,1},{1,0},{2,3},{3,2},{4,5},{5,4},{6,7},{7,6},{8,9},{9,8},{10,11... | collective-permute-start | bytes 319496 | tf_op jit(solution)/shard_map/ppermute | solution.py:397
  23.8 1.4 %collective-permute-start.13 = (f32[8,128]{1,0:T(8,128)S(1)}, f32[8,128]{1,0:T(8,128)S(1)}, u32[]{:S(2)}, u32[]{:S(2)}) collective-permute-start(f32[8,128]{1,0:T(8,128)S(1)} %add_add_fusion.refs_6_.refs_8_), channel_id=1, source_target_pairs={{0,1},{1,0},{2,3},{3,2},{4,5},{5,4},{6,7},{7,6},{8,9},{9,8},{10,11... | collective-permute-start | bytes 12296 | tf_op jit(solution)/shard_map/ppermute | solution.py:397

commit v3 on v2

--- a/solution.py
+++ b/solution.py
@@ -58,34 +58,23 @@
 
 
 def base_kernel(*refs):
-    sources, out_ref, targets, (keys, sems) = refs[:7], refs[7], refs[8:15], refs[15:]
+    sources, out_ref, targets, sems = refs[:5], refs[5], refs[6:11], refs[11]
     copies = [
         pltpu.make_async_copy(source, target, sems.at[i])
         for i, (source, target) in enumerate(zip(sources, targets))
     ]
     for copy in copies:
         copy.start()
-    image_ref, row_src, row_wt, col_src, col_wt, owner_ref, target_ref = targets
-    for copy in copies[1:]:
-        copy.wait()
+    image_ref, row_src, row_wt, col_src, col_wt = targets
     count, edge, _ = image_ref.shape
     rows = count * edge
     part = rows // 4
-    keys[...] = jnp.full(keys.shape, -1.0, F32)
+    for copy in copies[1:]:
+        copy.wait()
     row_ts, col_ts = [], []
     for p in range(count):
         row_ts.append(warp_matrix_t(row_src[p : p + 1, :], row_wt[p : p + 1, :], edge))
         col_ts.append(warp_matrix_t(col_src[p : p + 1, :], col_wt[p : p + 1, :], edge))
-    key = owner_ref[...] * rows + target_ref[...]
-    keys[0:1, 0:rows] = (key >> 8).astype(F32)
-    keys[8:9, 0:rows] = (key & 255).astype(F32)
-    wide = keys.shape[1] // LANES
-    blank = jnp.full((8 - wide, LANES), -1.0, F32)
-    lines = []
-    for half in (0, 8):
-        lines += [keys[half : half + 1, j * LANES : (j + 1) * LANES] for j in range(wide)]
-        lines += [blank]
-    out_ref[rows + part :, :] = jnp.concatenate(lines, axis=0).astype(BF16)
     copies[0].wait()
     pieces = []
     for p in range(count):
@@ -97,6 +86,21 @@
         right = base[:, LANES:]
         pieces += [right[:part], right[part:]]
     out_ref[rows : rows + part, :] = jnp.concatenate(pieces, axis=1).astype(BF16)
+
+
+def landing_rows(owner_ref, target_ref, keys):
+    rows = owner_ref.shape[1]
+    keys[...] = jnp.full(keys.shape, -1.0, F32)
+    key = owner_ref[...] * rows + target_ref[...]
+    keys[0:1, 0:rows] = (key >> 8).astype(F32)
+    keys[8:9, 0:rows] = (key & 255).astype(F32)
+    wide = keys.shape[1] // LANES
+    blank = jnp.full((8 - wide, LANES), -1.0, F32)
+    lines = []
+    for half in (0, 8):
+        lines += [keys[half : half + 1, j * LANES : (j + 1) * LANES] for j in range(wide)]
+        lines += [blank]
+    return jnp.concatenate(lines, axis=0).astype(BF16)
 
 
 def spectrum_of(pixels, dft_cos, dft_sin, count, edge):
@@ -120,17 +124,22 @@
     cos_ref,
     sin_ref,
     peaks_ref,
-    message_ref,
+    base_ref,
+    owner_ref,
+    target_ref,
     re_ref,
     im_ref,
     cos_row,
     sin_row,
     cos_col,
     sin_col,
-    copied_ref,
+    message_ref,
+    keys,
 ):
     count, edge, _ = image_ref.shape
-    copied_ref[...] = message_ref[...]
+    based = base_ref.shape[0]
+    message_ref[0:based, :] = base_ref[...]
+    message_ref[based:, :] = landing_rows(owner_ref, target_ref, keys)
     dft_cos, dft_sin = cos_ref[...], sin_ref[...]
     pixels = image_ref[...].reshape(count * edge, edge)
     spectra = spectrum_of(pixels, dft_cos, dft_sin, count, edge)
@@ -185,17 +194,24 @@
     pixels = jnp.concatenate(groups, axis=0)
     pixels = jnp.where(lax.axis_index("sec") > 0, pixels, 0.0).astype(BF16)
     spectra = spectrum_of(pixels, dft_cos, dft_sin, count, edge)
-    total = None
+    cross = []
     for p, (ref_re, ref_im) in enumerate(spectra):
         img_re, img_im = im_re_ref[p], im_im_ref[p]
         cross_re = (ref_re * img_re + ref_im * img_im).astype(BF16)
         cross_im = (ref_im * img_re - ref_re * img_im).astype(BF16)
+        cross.append((cross_re, cross_im))
+    back = []
+    for p, (cross_re, cross_im) in enumerate(cross):
+        back_re = (product(cross_re, cos_col[p]) - product(cross_im, sin_col[p])).astype(BF16)
+        back_im = (product(cross_re, sin_col[p]) + product(cross_im, cos_col[p])).astype(BF16)
+        back.append((back_re, back_im))
+    total = None
+    for p, (back_re, back_im) in enumerate(back):
+        near = product(cos_row[p], back_re) - product(sin_row[p], back_im)
+        total = near if total is None else total + near
+    for p, (cross_re, cross_im) in enumerate(cross):
         cross_re_ref[p] = cross_re
         cross_im_ref[p] = cross_im
-        back_re = (product(cross_re, cos_col[p]) - product(cross_im, sin_col[p])).astype(BF16)
-        back_im = (product(cross_re, sin_col[p]) + product(cross_im, cos_col[p])).astype(BF16)
-        near = product(cos_row[p], back_re) - product(sin_row[p], back_im)
-        total = near if total is None else total + near
     near_ref[...] = total[0:8] * (1.0 / (edge * edge))
 
 
@@ -408,40 +424,33 @@
     length = message_rows(rows)
     wide = round_up(rows, LANES)
 
-    inputs = (
-        pixels,
-        row_source[0],
-        row_weight[0],
-        col_source[0],
-        col_weight[0],
-        owner[0].reshape(1, rows),
-        render_row,
-    )
-    message = call(
+    inputs = (pixels, row_source[0], row_weight[0], col_source[0], col_weight[0])
+    base = call(
         base_kernel,
-        jax.ShapeDtypeStruct((length, LANES), BF16),
+        jax.ShapeDtypeStruct((length - 16, LANES), BF16),
         len(inputs),
         space=pltpu.HBM,
         scratch=[pltpu.VMEM(x.shape, x.dtype) for x in inputs]
-        + [pltpu.VMEM((16, wide), F32), pltpu.SemaphoreType.DMA((len(inputs),))],
+        + [pltpu.SemaphoreType.DMA((len(inputs),))],
     )(*[pltpu.with_memory_space_constraint(x, pltpu.HBM) for x in inputs])
-    prior_message = turned(message, "sec", 1)
+    prior_base = turned(base, "sec", 1)
 
     def table(*shape, kind=BF16):
         return jax.ShapeDtypeStruct(shape, kind)
 
     square = table(count, edge, edge, kind=F32)
     slim, tall = table(count, 16, edge), table(count, edge, LANES)
-    *spectra, copied = call(
+    *spectra, message = call(
         spectrum_kernel,
         (square, square, slim, slim, tall, tall, table(length, LANES)),
-        5,
-    )(pixels, dft_cos, dft_sin, peaks[0], message)
+        7,
+        scratch=[pltpu.VMEM((16, wide), F32)],
+    )(pixels, dft_cos, dft_sin, peaks[0], base, owner[0].reshape(1, rows), render_row)
     near, cross_re, cross_im = call(
         near_kernel,
         (table(8, LANES, kind=F32), table(count, edge, edge), table(count, edge, edge)),
         9,
-    )(prior_message, *spectra[:2], dft_cos, dft_sin, *spectra[2:])
+    )(prior_base, *spectra[:2], dft_cos, dft_sin, *spectra[2:])
 
     surfaces = call(surface_kernel, (square,) * 3, 4)(cross_re, cross_im, dft_cos, dft_sin)
 
@@ -455,14 +464,14 @@
     def stack(slots):
         return pltpu.VMEM((round_up(slots * rows, LANES), 2 * LANES), BF16)
 
-    few = strips <= 8 and strips & (strips - 1) == 0
+    few = strips == 8
     order = [surfaces[0]]
     if few:
         offsets = [2 * k for k in range(strips // 2)]
-        blocks = [copied]
+        blocks = [message]
         for offset in offsets[1:]:
             far = 1 << offset.bit_length() - 1
-            blocks.append(swapped(copied, far) if offset == far else swapped(blocks[far // 2], offset - far))
+            blocks.append(swapped(message, far) if offset == far else swapped(blocks[far // 2], offset - far))
 
         def prepared(group, after):
             return call(
@@ -472,7 +481,7 @@
                 scratch=[key_line(len(group))],
             )(*group, after)
 
-        early_side = prepared([copied, swapped(message, 1)], near)
+        early_side = prepared([message, swapped(message, 1)], near)
         order.append(early_side[0])
 
     nears = [near] + [turned(near, "sec", k) for k in range(1, sections - 1)]
@@ -504,7 +513,7 @@
             2,
             scratch=[pltpu.VMEM(x.shape, x.dtype) for x in laid(1)] + [key_line(1), stack(1)],
             vmem=2 * strips * length * LANES * 2 + VMEM_BYTES,
-        )(lax.all_gather(copied, "strip"), lax.psum(passed, "strip"))
+        )(lax.all_gather(message, "strip"), lax.psum(passed, "strip"))
     return (render.T[None], corr_map[None])
 
 

time: 26.9 us -> 27 us (level)
  transfers between devices with their start and end apart: 14 -> 14, of which waited for: 4 -> 6; matrix products, arithmetic and copies ran while one was open for 0% -> 0% of each run, Pallas kernels for 20% -> 19%
where the time goes in v3:
time: 27 us; the launch traced here: 26.8 us
  starting transfers between devices  14.8 us (55%)
  Pallas kernels  8.4 us (31%)
  waiting for transfers between devices  2.83 us (10%)
  between operations  0.79 us (3%)
    ppermute x11, starting transfers between devices, swapped(): lax.ppermute(block, 'strip', [(i, i ^ offset) for i in range(lax.axis_siz...  9.74 us
    ppermute x3, starting transfers between devices, turned(): lax.ppermute(block, axis, [(i, (i + distance) % size) for i in range(size)])  5.03 us
    ppermute x11, waiting for transfers between devices, swapped(): lax.ppermute(block, 'strip', [(i, i ^ offset) for i in range(lax.axis_siz...  2.82 us
    pallas_call x1, Pallas kernels, on_device(): call(functools.partial(render_kernel, count, edge, groups), rendered, 10,...  1.64 us
    pallas_call x1, Pallas kernels, on_device(): call(base_kernel, jax.ShapeDtypeStruct((length - 16, LANES), BF16), len(i...  1.61 us
    pallas_call x2, Pallas kernels, prepared(): call(functools.partial(prepare_kernel, count, edge, len(group)), laid(len...  1.37 us
    pallas_call x1, Pallas kernels, on_device(): call(map_kernel, (square, table(8, patches_all, kind=F32)), 5)  0.86 us
    pallas_call x1, Pallas kernels, on_device(): call(surface_kernel, (square,) * 3, 4)(cross_re, cross_im, dft_cos, dft_sin)  0.85 us
  transfers between devices with their start and end apart: 14, of which 6 were waited for; matrix products, arithmetic and copies ran while one was open for 0% of the time, Pallas kernels for 19%

profile of v3, /device:TPU:0, one launch (start us, length us, event | category | flops | bytes accessed | tf_op | source)
XLA Modules:
  0.0 26.8 jit_solution(14873712919432728075)
XLA Ops:
  0.6 0.0 copy-start
  0.6 0.0 copy-start.1
  0.7 0.0 copy-start.2
  0.7 0.0 copy-start.3
  0.7 0.0 copy-start.4
  0.7 0.0 copy-start.5
  0.7 1.6 %shard_map.113.base_ref = bf16[400,128]{1,0:T(8,128)(2,1)S(1)} custom-call(bf16[2,160,160]{2,1,0:T(8,128)(2,1)} %bitcast.11, s32[2,160]{1,0:T(2,128)} %bitcast.16, f32[2,160]{1,0:T(2,128)} %bitcast.17, s32[2,160]{1,0:T(2,128)} %bitcast.18, f32[2,160]{1,0:T(2,128)} %bitcast.19), custom_call_target="tpu_custom_call" | custom-call | flops 1000000000 | bytes 500000 | tf_op jit(solution)/shard_map/pallas_call | solution.py:428
  2.3 3.0 %collective-permute-start.1 = (bf16[400,128]{1,0:T(8,128)(2,1)S(1)}, bf16[400,128]{1,0:T(8,128)(2,1)S(1)}, u32[]{:S(2)}, u32[]{:S(2)}) collective-permute-start(bf16[400,128]{1,0:T(8,128)(2,1)S(1)} %shard_map.113.base_ref), channel_id=1, source_target_pairs={{0,8},{8,16},{16,24},{24,0},{1,9},{9,17},{17,25},{25,1},{2,10},{10... | collective-permute-start | bytes 307208 | tf_op jit(solution)/shard_map/ppermute | solution.py:409
  5.3 0.0 copy-done
  5.3 0.0 copy-done.1
  5.3 0.0 copy-done.2
  5.3 0.0 copy-done.3
  5.3 0.0 copy-done.4
  5.3 0.0 copy-done.5
  5.3 0.7 %shard_map.114 = (f32[2,160,160]{2,1,0:T(8,128)S(1)}, f32[2,160,160]{2,1,0:T(8,128)S(1)}, bf16[2,16,160]{2,1,0:T(8,128)(2,1)S(1)}, bf16[2,16,160]{2,1,0:T(8,128)...) custom-call(bf16[2,160,160]{2,1,0:T(8,128)(2,1)S(1)} %bitcast.12, ...), custom_call_target="tpu_custom_call" | custom-call | flops 1000000000 | bytes 500000 | tf_op jit(solution)/shard_map/pallas_call | solution.py:443
  6.0 0.1 collective-permute-start
  6.1 1.6 %collective-permute-start.2 = (bf16[416,128]{1,0:T(8,128)(2,1)S(1)}, bf16[416,128]{1,0:T(8,128)(2,1)S(1)}, u32[]{:S(2)}, u32[]{:S(2)}) collective-permute-start(bf16[416,128]{1,0:T(8,128)(2,1)S(1)} %get-tuple-element.27.refs_0_), channel_id=1, source_target_pairs={{0,2},{1,3},{2,0},{3,1},{4,6},{5,7},{6,4},{7,5},{8,10},{9,11},{10,... | collective-permute-start | bytes 319496 | tf_op jit(solution)/shard_map/ppermute | solution.py:413
  7.7 2.6 %collective-permute-start.3 = (bf16[416,128]{1,0:T(8,128)(2,1)S(1)}, bf16[416,128]{1,0:T(8,128)(2,1)S(1)}, u32[]{:S(2)}, u32[]{:S(2)}) collective-permute-start(bf16[416,128]{1,0:T(8,128)(2,1)S(1)} %get-tuple-element.27.refs_0_), channel_id=1, source_target_pairs={{0,4},{1,5},{2,6},{3,7},{4,0},{5,1},{6,2},{7,3},{8,12},{9,13},{10,... | collective-permute-start | bytes 319496 | tf_op jit(solution)/shard_map/ppermute | solution.py:413
  10.3 0.0 collective-permute-done.1.message_ref
  10.3 0.8 %shard_map.115 = (f32[8,128]{1,0:T(8,128)S(1)}, bf16[2,160,160]{2,1,0:T(8,128)(2,1)S(1)}, bf16[2,160,160]{2,1,0:T(8,128)(2,1)S(1)}) custom-call(bf16[400,128]{1,0:T(8,128)(2,1)S(1)} %collective-permute-done.1.message_ref, f32[2,160,160]{2,1,0:T(8,128)S(1)} %get-tuple-element.28.im_re_ref, f32[2,160,160]{2,1,0:T(8,128)S(1)} %get-tuple-element.29.im_im_ref, ...), custom_call_target="tpu_custom_call" | custom-call | flops 1000000000 | bytes 500000 | tf_op jit(solution)/shard_map/pallas_call | solution.py:449
  11.2 1.5 %collective-permute-start.8 = (f32[8,128]{1,0:T(8,128)S(1)}, f32[8,128]{1,0:T(8,128)S(1)}, u32[]{:S(2)}, u32[]{:S(2)}) collective-permute-start(f32[8,128]{1,0:T(8,128)S(1)} %get-tuple-element.34.refs_2_.refs_0_), channel_id=1, source_target_pairs={{0,8},{8,16},{16,24},{24,0},{1,9},{9,17},{17,25},{25,1},{2,10},{10... | collective-permute-start | bytes 12296 | tf_op jit(solution)/shard_map/ppermute | solution.py:409
  12.7 0.5 %collective-permute-start.9 = (f32[8,128]{1,0:T(8,128)S(1)}, f32[8,128]{1,0:T(8,128)S(1)}, u32[]{:S(2)}, u32[]{:S(2)}) collective-permute-start(f32[8,128]{1,0:T(8,128)S(1)} %get-tuple-element.34.refs_2_.refs_0_), channel_id=1, source_target_pairs={{0,16},{8,24},{16,0},{24,8},{1,17},{9,25},{17,1},{25,9},{2,18},{10... | collective-permute-start | bytes 12296 | tf_op jit(solution)/shard_map/ppermute | solution.py:409
  13.2 0.8 %shard_map.117 = (f32[2,160,160]{2,1,0:T(8,128)S(1)}, f32[2,160,160]{2,1,0:T(8,128)S(1)}, f32[2,160,160]{2,1,0:T(8,128)S(1)}) custom-call(bf16[2,160,160]{2,1,0:T(8,128)(2,1)S(1)} %get-tuple-element.39.cross_re_ref, bf16[2,160,160]{2,1,0:T(8,128)(2,1)S(1)} %get-tuple-element.40.cross_im_ref, bf16[160,160]{1,0:T(8,128)(2,1)S(1)} %copy-done.4, ...), custom_call_target="tpu_custom_call" | custom-call | flops 1000000000 | bytes 500000 | tf_op jit(solution)/shard_map/pallas_call | solution.py:455
  14.1 0.0 collective-permute-done.refs_1_
  14.1 0.4 %shard_map.116 = (bf16[320,640]{1,0:T(8,128)(2,1)S(1)}, bf16[640,256]{1,0:T(8,128)(2,1)S(1)}, bf16[640,256]{1,0:T(8,128)(2,1)S(1)}, bf16[640,256]{1,0:T(8,128)(2,1)S(1)}) custom-call(bf16[416,128]{1,0:T(8,128)(2,1)S(1)} %get-tuple-element.27.refs_0_, bf16[416,128]{1,0:T(8,128)(2,1)S(1)} %collective-permute-done.refs_1_, ...), custom_call_target="tpu_custom_call" | custom-call | flops 1000000000 | bytes 500000 | tf_op jit(solution)/shard_map/pallas_call | solution.py:477
  14.5 1.5 %collective-permute-done.3.refs_1_ = bf16[416,128]{1,0:T(8,128)(2,1)S(1)} collective-permute-done((bf16[416,128]{1,0:T(8,128)(2,1)S(1)}, bf16[416,128]{1,0:T(8,128)(2,1)S(1)}, u32[]{:S(2)}, u32[]{:S(2)}) %collective-permute-start.3) | collective-permute-done | bytes 106528 | tf_op jit(solution)/shard_map/ppermute | solution.py:413
  16.0 0.5 %collective-permute-start.4 = (bf16[416,128]{1,0:T(8,128)(2,1)S(1)}, bf16[416,128]{1,0:T(8,128)(2,1)S(1)}, u32[]{:S(2)}, u32[]{:S(2)}) collective-permute-start(bf16[416,128]{1,0:T(8,128)(2,1)S(1)} %collective-permute-done.3.refs_1_), channel_id=1, source_target_pairs={{0,2},{1,3},{2,0},{3,1},{4,6},{5,7},{6,4},{7,5},{8,10},{9,11},{10,... | collective-permute-start | bytes 319496 | tf_op jit(solution)/shard_map/ppermute | solution.py:413
  16.5 0.0 collective-permute-done.8.refs_1_
  16.5 0.0 collective-permute-done.9.refs_2_
  16.5 0.6 %shard_map.118 = (f32[8,128]{1,0:T(8,128)S(1)}, f32[8,128]{1,0:T(8,128)S(1)}) custom-call(f32[8,128]{1,0:T(8,128)S(1)} %get-tuple-element.34.refs_2_.refs_0_, f32[8,128]{1,0:T(8,128)S(1)} %collective-permute-done.8.refs_1_, f32[8,128]{1,0:T(8,128)S(1)} %collective-permute-done.9.refs_2_, f32[2,160,160]{2,1,0:T(8,128)S(1)} %get-tuple-element.41.refs_3_.corr_ref, ...), custom_call_target="tpu_custom_call" | custom-call | flops 1000000000 | bytes 500000 | tf_op jit(solution)/shard_map/pallas_call | solution.py:489
  17.0 2.1 %collective-permute-start.12 = (f32[8,128]{1,0:T(8,128)S(1)}, f32[8,128]{1,0:T(8,128)S(1)}, u32[]{:S(2)}, u32[]{:S(2)}) collective-permute-start(f32[8,128]{1,0:T(8,128)S(1)} %get-tuple-element.45.smooth_ref), channel_id=1, source_target_pairs={{0,6},{1,7},{2,4},{3,5},{4,2},{5,3},{6,0},{7,1},{8,14},{9,15},{10,... | collective-permute-start | bytes 12296 | tf_op jit(solution)/shard_map/ppermute | solution.py:413
  19.1 1.0 %collective-permute-start.11 = (f32[8,128]{1,0:T(8,128)S(1)}, f32[8,128]{1,0:T(8,128)S(1)}, u32[]{:S(2)}, u32[]{:S(2)}) collective-permute-start(f32[8,128]{1,0:T(8,128)S(1)} %get-tuple-element.45.smooth_ref), channel_id=1, source_target_pairs={{0,4},{1,5},{2,6},{3,7},{4,0},{5,1},{6,2},{7,3},{8,12},{9,13},{10,... | collective-permute-start | bytes 12296 | tf_op jit(solution)/shard_map/ppermute | solution.py:413
  20.1 1.4 %collective-permute-start.10 = (f32[8,128]{1,0:T(8,128)S(1)}, f32[8,128]{1,0:T(8,128)S(1)}, u32[]{:S(2)}, u32[]{:S(2)}) collective-permute-start(f32[8,128]{1,0:T(8,128)S(1)} %get-tuple-element.45.smooth_ref), channel_id=1, source_target_pairs={{0,2},{1,3},{2,0},{3,1},{4,6},{5,7},{6,4},{7,5},{8,10},{9,11},{10,... | collective-permute-start | bytes 12296 | tf_op jit(solution)/shard_map/ppermute | solution.py:413
  21.5 0.9 %shard_map.119 = (f32[2,160,160]{2,1,0:T(8,128)}, f32[8,128]{1,0:T(8,128)S(1)}) custom-call(f32[2,160,160]{2,1,0:T(8,128)S(1)} %get-tuple-element.41.refs_3_.corr_ref, f32[2,160,160]{2,1,0:T(8,128)S(1)} %get-tuple-element.42.grad_y_ref, f32[2,160,160]{2,1,0:T(8,128)S(1)} %get-tuple-element.43.grad_x_ref, f32[8,128]{1,0:T(8,128)S(1)} %get-tuple-element.44.prior_ref, ...), custom_call_target="tpu_custom_call" | custom-call | flops 1000000000 | bytes 500000 | tf_op jit(solution)/shard_map/pallas_call | solution.py:494
  22.4 0.0 collective-permute-done.2.refs_0_
  22.4 0.0 collective-permute-start.6
  22.4 0.1 collective-permute-done.12
  22.5 0.4 %collective-permute-start.5 = (bf16[416,128]{1,0:T(8,128)(2,1)S(1)}, bf16[416,128]{1,0:T(8,128)(2,1)S(1)}, u32[]{:S(2)}, u32[]{:S(2)}) collective-permute-start(bf16[416,128]{1,0:T(8,128)(2,1)S(1)} %collective-permute-done.2.refs_0_), channel_id=1, source_target_pairs={{0,1},{1,0},{2,3},{3,2},{4,5},{5,4},{6,7},{7,6},{8,9},{9,8},{10,11... | collective-permute-start | bytes 319496 | tf_op jit(solution)/shard_map/ppermute | solution.py:413
  22.9 0.0 collective-permute-done.4.refs_2_
  22.9 0.1 collective-permute-start.7
  23.0 0.6 %collective-permute-done.11 = f32[8,128]{1,0:T(8,128)S(1)} collective-permute-done((f32[8,128]{1,0:T(8,128)S(1)}, f32[8,128]{1,0:T(8,128)S(1)}, u32[]{:S(2)}, u32[]{:S(2)}) %collective-permute-start.11) | collective-permute-done | bytes 4128 | tf_op jit(solution)/shard_map/ppermute | solution.py:413
  23.6 0.1 collective-permute-done.10
  23.7 0.0 collective-permute-start.13
  23.8 0.1 collective-permute-done.5.refs_3_
  23.8 0.0 collective-permute-done.6.refs_4_
  23.8 0.4 %collective-permute-done.7.refs_5_ = bf16[416,128]{1,0:T(8,128)(2,1)S(1)} collective-permute-done((bf16[416,128]{1,0:T(8,128)(2,1)S(1)}, bf16[416,128]{1,0:T(8,128)(2,1)S(1)}, u32[]{:S(2)}, u32[]{:S(2)}) %collective-permute-start.7) | collective-permute-done | bytes 106528 | tf_op jit(solution)/shard_map/ppermute | solution.py:413
  24.2 1.0 %shard_map.120 = (bf16[320,1920]{1,0:T(8,128)(2,1)S(1)}, bf16[1920,256]{1,0:T(8,128)(2,1)S(1)}, bf16[1920,256]{1,0:T(8,128)(2,1)S(1)}, bf16[1920,256]{1,0:T(8,128)(2,1)S(1)}) custom-call(bf16[416,128]{1,0:T(8,128)(2,1)S(1)} %collective-permute-done.2.refs_0_, bf16[416,128]{1,0:T(8,128)(2,1)S(1)} %collective-permute-done.3.refs_1_, ...), custom_call_target="tpu_custom_call" | custom-call | flops 1000000000 | bytes 500000 | tf_op jit(solution)/shard_map/pallas_call | solution.py:477
  25.2 0.0 collective-permute-done.13.refs_9_
  25.2 1.6 %shard_map.121 = bf16[160,320]{1,0:T(8,128)(2,1)} custom-call(bf16[320,640]{1,0:T(8,128)(2,1)S(1)} %get-tuple-element.35.refs_4_.refs_0_, bf16[640,256]{1,0:T(8,128)(2,1)S(1)} %get-tuple-element.36.refs_1_, bf16[640,256]{1,0:T(8,128)(2,1)S(1)} %get-tuple-element.37.refs_2_, bf16[640,256]{1,0:T(8,128)(2,1)S(1)} %get-tuple-element.38.refs_3_, ...), custom_call_target="tpu_custom_call" | custom-call | flops 1000000000 | bytes 500000 | tf_op jit(solution)/shard_map/pallas_call | solution.py:503
  (1 shorter events, 0.0 us)
Async XLA Ops:
  0.6 4.7 %copy-start = (bf16[1,2,160,160]{3,2,1,0:T(8,128)(2,1)S(1)}, bf16[1,2,160,160]{3,2,1,0:T(8,128)(2,1)}, u32[]{:S(2)}) copy-start(bf16[1,2,160,160]{3,2,1,0:T(8,128)(2,1)} %param.10) | copy-start | bytes 307204
  0.6 4.7 %copy-start.1 = (s32[1,320,1]{1,2,0:T(1,128)S(1)}, s32[1,320,1]{1,2,0:T(1,128)}, u32[]{:S(2)}) copy-start(s32[1,320,1]{1,2,0:T(1,128)} %param.16) | copy-start | bytes 3844
  0.7 4.7 %copy-start.2 = (s32[1,320]{1,0:T(1,128)S(1)}, s32[1,320]{1,0:T(1,128)}, u32[]{:S(2)}) copy-start(s32[1,320]{1,0:T(1,128)} %target_ref.1) | copy-start | bytes 3844
  0.7 4.7 %copy-start.3 = (s32[1,2,2]{2,1,0:T(2,128)S(1)}, s32[1,2,2]{2,1,0:T(2,128)}, u32[]{:S(2)}) copy-start(s32[1,2,2]{2,1,0:T(2,128)} %param.11) | copy-start | bytes 52
  0.7 4.7 %copy-start.4 = (bf16[160,160]{1,0:T(8,128)(2,1)S(1)}, bf16[160,160]{1,0:T(8,128)(2,1)}, u32[]{:S(2)}) copy-start(bf16[160,160]{1,0:T(8,128)(2,1)} %constant.4.clone.cos_ref) | copy-start | bytes 153604
  0.7 4.7 %copy-start.5 = (bf16[160,160]{1,0:T(8,128)(2,1)S(1)}, bf16[160,160]{1,0:T(8,128)(2,1)}, u32[]{:S(2)}) copy-start(bf16[160,160]{1,0:T(8,128)(2,1)} %constant.5.clone.sin_ref) | copy-start | bytes 153604
  2.3 8.0 %collective-permute-start.1 = (bf16[400,128]{1,0:T(8,128)(2,1)S(1)}, bf16[400,128]{1,0:T(8,128)(2,1)S(1)}, u32[]{:S(2)}, u32[]{:S(2)}) collective-permute-start(bf16[400,128]{1,0:T(8,128)(2,1)S(1)} %shard_map.113.base_ref), channel_id=1, source_target_pairs={{0,8},{8,16},{16,24},{24,0},{1,9},{9,17},{17,25},{25,1},{2,10},{10... | collective-permute-start | bytes 307208 | tf_op jit(solution)/shard_map/ppermute | solution.py:409
  6.0 8.0 %collective-permute-start = (bf16[416,128]{1,0:T(8,128)(2,1)S(1)}, bf16[416,128]{1,0:T(8,128)(2,1)S(1)}, u32[]{:S(2)}, u32[]{:S(2)}) collective-permute-start(bf16[416,128]{1,0:T(8,128)(2,1)S(1)} %get-tuple-element.27.refs_0_), channel_id=1, source_target_pairs={{0,1},{1,0},{2,3},{3,2},{4,5},{5,4},{6,7},{7,6},{8,9},{9,8},{10,11... | collective-permute-start | bytes 319496 | tf_op jit(solution)/shard_map/ppermute | solution.py:413
  6.1 16.3 %collective-permute-start.2 = (bf16[416,128]{1,0:T(8,128)(2,1)S(1)}, bf16[416,128]{1,0:T(8,128)(2,1)S(1)}, u32[]{:S(2)}, u32[]{:S(2)}) collective-permute-start(bf16[416,128]{1,0:T(8,128)(2,1)S(1)} %get-tuple-element.27.refs_0_), channel_id=1, source_target_pairs={{0,2},{1,3},{2,0},{3,1},{4,6},{5,7},{6,4},{7,5},{8,10},{9,11},{10,... | collective-permute-start | bytes 319496 | tf_op jit(solution)/shard_map/ppermute | solution.py:413
  7.7 8.3 %collective-permute-start.3 = (bf16[416,128]{1,0:T(8,128)(2,1)S(1)}, bf16[416,128]{1,0:T(8,128)(2,1)S(1)}, u32[]{:S(2)}, u32[]{:S(2)}) collective-permute-start(bf16[416,128]{1,0:T(8,128)(2,1)S(1)} %get-tuple-element.27.refs_0_), channel_id=1, source_target_pairs={{0,4},{1,5},{2,6},{3,7},{4,0},{5,1},{6,2},{7,3},{8,12},{9,13},{10,... | collective-permute-start | bytes 319496 | tf_op jit(solution)/shard_map/ppermute | solution.py:413
  11.2 5.3 %collective-permute-start.8 = (f32[8,128]{1,0:T(8,128)S(1)}, f32[8,128]{1,0:T(8,128)S(1)}, u32[]{:S(2)}, u32[]{:S(2)}) collective-permute-start(f32[8,128]{1,0:T(8,128)S(1)} %get-tuple-element.34.refs_2_.refs_0_), channel_id=1, source_target_pairs={{0,8},{8,16},{16,24},{24,0},{1,9},{9,17},{17,25},{25,1},{2,10},{10... | collective-permute-start | bytes 12296 | tf_op jit(solution)/shard_map/ppermute | solution.py:409
  12.7 3.8 %collective-permute-start.9 = (f32[8,128]{1,0:T(8,128)S(1)}, f32[8,128]{1,0:T(8,128)S(1)}, u32[]{:S(2)}, u32[]{:S(2)}) collective-permute-start(f32[8,128]{1,0:T(8,128)S(1)} %get-tuple-element.34.refs_2_.refs_0_), channel_id=1, source_target_pairs={{0,16},{8,24},{16,0},{24,8},{1,17},{9,25},{17,1},{25,9},{2,18},{10... | collective-permute-start | bytes 12296 | tf_op jit(solution)/shard_map/ppermute | solution.py:409
  16.0 6.9 %collective-permute-start.4 = (bf16[416,128]{1,0:T(8,128)(2,1)S(1)}, bf16[416,128]{1,0:T(8,128)(2,1)S(1)}, u32[]{:S(2)}, u32[]{:S(2)}) collective-permute-start(bf16[416,128]{1,0:T(8,128)(2,1)S(1)} %collective-permute-done.3.refs_1_), channel_id=1, source_target_pairs={{0,2},{1,3},{2,0},{3,1},{4,6},{5,7},{6,4},{7,5},{8,10},{9,11},{10,... | collective-permute-start | bytes 319496 | tf_op jit(solution)/shard_map/ppermute | solution.py:413
  17.0 5.5 %collective-permute-start.12 = (f32[8,128]{1,0:T(8,128)S(1)}, f32[8,128]{1,0:T(8,128)S(1)}, u32[]{:S(2)}, u32[]{:S(2)}) collective-permute-start(f32[8,128]{1,0:T(8,128)S(1)} %get-tuple-element.45.smooth_ref), channel_id=1, source_target_pairs={{0,6},{1,7},{2,4},{3,5},{4,2},{5,3},{6,0},{7,1},{8,14},{9,15},{10,... | collective-permute-start | bytes 12296 | tf_op jit(solution)/shard_map/ppermute | solution.py:413
  19.1 4.5 %collective-permute-start.11 = (f32[8,128]{1,0:T(8,128)S(1)}, f32[8,128]{1,0:T(8,128)S(1)}, u32[]{:S(2)}, u32[]{:S(2)}) collective-permute-start(f32[8,128]{1,0:T(8,128)S(1)} %get-tuple-element.45.smooth_ref), channel_id=1, source_target_pairs={{0,4},{1,5},{2,6},{3,7},{4,0},{5,1},{6,2},{7,3},{8,12},{9,13},{10,... | collective-permute-start | bytes 12296 | tf_op jit(solution)/shard_map/ppermute | solution.py:413
  20.1 3.6 %collective-permute-start.10 = (f32[8,128]{1,0:T(8,128)S(1)}, f32[8,128]{1,0:T(8,128)S(1)}, u32[]{:S(2)}, u32[]{:S(2)}) collective-permute-start(f32[8,128]{1,0:T(8,128)S(1)} %get-tuple-element.45.smooth_ref), channel_id=1, source_target_pairs={{0,2},{1,3},{2,0},{3,1},{4,6},{5,7},{6,4},{7,5},{8,10},{9,11},{10,... | collective-permute-start | bytes 12296 | tf_op jit(solution)/shard_map/ppermute | solution.py:413
  22.4 1.5 %collective-permute-start.6 = (bf16[416,128]{1,0:T(8,128)(2,1)S(1)}, bf16[416,128]{1,0:T(8,128)(2,1)S(1)}, u32[]{:S(2)}, u32[]{:S(2)}) collective-permute-start(bf16[416,128]{1,0:T(8,128)(2,1)S(1)} %collective-permute-done.3.refs_1_), channel_id=1, source_target_pairs={{0,1},{1,0},{2,3},{3,2},{4,5},{5,4},{6,7},{7,6},{8,9},{9,8},{10,11... | collective-permute-start | bytes 319496 | tf_op jit(solution)/shard_map/ppermute | solution.py:413
  22.5 1.3 %collective-permute-start.5 = (bf16[416,128]{1,0:T(8,128)(2,1)S(1)}, bf16[416,128]{1,0:T(8,128)(2,1)S(1)}, u32[]{:S(2)}, u32[]{:S(2)}) collective-permute-start(bf16[416,128]{1,0:T(8,128)(2,1)S(1)} %collective-permute-done.2.refs_0_), channel_id=1, source_target_pairs={{0,1},{1,0},{2,3},{3,2},{4,5},{5,4},{6,7},{7,6},{8,9},{9,8},{10,11... | collective-permute-start | bytes 319496 | tf_op jit(solution)/shard_map/ppermute | solution.py:413
  22.9 1.3 %collective-permute-start.7 = (bf16[416,128]{1,0:T(8,128)(2,1)S(1)}, bf16[416,128]{1,0:T(8,128)(2,1)S(1)}, u32[]{:S(2)}, u32[]{:S(2)}) collective-permute-start(bf16[416,128]{1,0:T(8,128)(2,1)S(1)} %collective-permute-done.4.refs_2_), channel_id=1, source_target_pairs={{0,1},{1,0},{2,3},{3,2},{4,5},{5,4},{6,7},{7,6},{8,9},{9,8},{10,11... | collective-permute-start | bytes 319496 | tf_op jit(solution)/shard_map/ppermute | solution.py:413
  23.7 1.4 %collective-permute-start.13 = (f32[8,128]{1,0:T(8,128)S(1)}, f32[8,128]{1,0:T(8,128)S(1)}, u32[]{:S(2)}, u32[]{:S(2)}) collective-permute-start(f32[8,128]{1,0:T(8,128)S(1)} %add_add_fusion.refs_6_.refs_8_), channel_id=1, source_target_pairs={{0,1},{1,0},{2,3},{3,2},{4,5},{5,4},{6,7},{7,6},{8,9},{9,8},{10,11... | collective-permute-start | bytes 12296 | tf_op jit(solution)/shard_map/ppermute | solution.py:413

commit v4 on v3

--- a/solution.py
+++ b/solution.py
@@ -141,12 +141,6 @@
     message_ref[0:based, :] = base_ref[...]
     message_ref[based:, :] = landing_rows(owner_ref, target_ref, keys)
     dft_cos, dft_sin = cos_ref[...], sin_ref[...]
-    pixels = image_ref[...].reshape(count * edge, edge)
-    spectra = spectrum_of(pixels, dft_cos, dft_sin, count, edge)
-    for p, (s_re, s_im) in enumerate(spectra):
-        re_ref[p] = s_re
-        im_ref[p] = s_im
-
     def wrap(spot):
         return jnp.where(spot < 0, spot + edge, jnp.where(spot >= edge, spot - edge, spot))
 
@@ -165,6 +159,11 @@
         pick = jnp.where(jnp.logical_and(near, col == spot), 1.0, 0.0).astype(BF16)
         cos_col[p] = product(dft_cos, pick).astype(BF16)
         sin_col[p] = product(dft_sin, pick).astype(BF16)
+    pixels = image_ref[...].reshape(count * edge, edge)
+    spectra = spectrum_of(pixels, dft_cos, dft_sin, count, edge)
+    for p, (s_re, s_im) in enumerate(spectra):
+        re_ref[p] = s_re
+        im_ref[p] = s_im
 
 
 def near_kernel(

time: 27 us -> 27 us (level)
  no operation moved by 1% of the time
where the time goes in v4:
time: 27 us; the launch traced here: 26.9 us
  starting transfers between devices  14.7 us (54%)
  Pallas kernels  8.47 us (31%)
  waiting for transfers between devices  2.85 us (11%)
  between operations  0.79 us (3%)
    ppermute x11, starting transfers between devices, swapped(): lax.ppermute(block, 'strip', [(i, i ^ offset) for i in range(lax.axis_siz...  9.71 us
    ppermute x3, starting transfers between devices, turned(): lax.ppermute(block, axis, [(i, (i + distance) % size) for i in range(size)])  5.03 us
    ppermute x11, waiting for transfers between devices, swapped(): lax.ppermute(block, 'strip', [(i, i ^ offset) for i in range(lax.axis_siz...  2.84 us
    pallas_call x1, Pallas kernels, on_device(): call(functools.partial(render_kernel, count, edge, groups), rendered, 10,...  1.64 us
    pallas_call x1, Pallas kernels, on_device(): call(base_kernel, jax.ShapeDtypeStruct((length - 16, LANES), BF16), len(i...  1.61 us
    pallas_call x2, Pallas kernels, prepared(): call(functools.partial(prepare_kernel, count, edge, len(group)), laid(len...  1.36 us
    pallas_call x1, Pallas kernels, on_device(): call(map_kernel, (square, table(8, patches_all, kind=F32)), 5)  0.86 us
    pallas_call x1, Pallas kernels, on_device(): call(surface_kernel, (square,) * 3, 4)(cross_re, cross_im, dft_cos, dft_sin)  0.85 us
  transfers between devices with their start and end apart: 14, of which 6 were waited for; matrix products, arithmetic and copies ran while one was open for 0% of the time, Pallas kernels for 19%

profile of v4, /device:TPU:0, one launch (start us, length us, event | category | flops | bytes accessed | tf_op | source)
XLA Modules:
  0.0 26.9 jit_solution(12819808788775235164)
XLA Ops:
  0.6 0.0 copy-start
  0.6 0.0 copy-start.1
  0.7 0.0 copy-start.2
  0.7 0.0 copy-start.3
  0.7 0.0 copy-start.4
  0.7 0.0 copy-start.5
  0.7 1.6 %shard_map.113.base_ref = bf16[400,128]{1,0:T(8,128)(2,1)S(1)} custom-call(bf16[2,160,160]{2,1,0:T(8,128)(2,1)} %bitcast.11, s32[2,160]{1,0:T(2,128)} %bitcast.16, f32[2,160]{1,0:T(2,128)} %bitcast.17, s32[2,160]{1,0:T(2,128)} %bitcast.18, f32[2,160]{1,0:T(2,128)} %bitcast.19), custom_call_target="tpu_custom_call" | custom-call | flops 1000000000 | bytes 500000 | tf_op jit(solution)/shard_map/pallas_call | solution.py:427
  2.3 3.0 %collective-permute-start.1 = (bf16[400,128]{1,0:T(8,128)(2,1)S(1)}, bf16[400,128]{1,0:T(8,128)(2,1)S(1)}, u32[]{:S(2)}, u32[]{:S(2)}) collective-permute-start(bf16[400,128]{1,0:T(8,128)(2,1)S(1)} %shard_map.113.base_ref), channel_id=1, source_target_pairs={{0,8},{8,16},{16,24},{24,0},{1,9},{9,17},{17,25},{25,1},{2,10},{10... | collective-permute-start | bytes 307208 | tf_op jit(solution)/shard_map/ppermute | solution.py:408
  5.3 0.0 copy-done
  5.3 0.0 copy-done.1
  5.3 0.0 copy-done.2
  5.3 0.0 copy-done.3
  5.3 0.0 copy-done.4
  5.3 0.0 copy-done.5
  5.3 0.7 %shard_map.114 = (f32[2,160,160]{2,1,0:T(8,128)S(1)}, f32[2,160,160]{2,1,0:T(8,128)S(1)}, bf16[2,16,160]{2,1,0:T(8,128)(2,1)S(1)}, bf16[2,16,160]{2,1,0:T(8,128)...) custom-call(bf16[2,160,160]{2,1,0:T(8,128)(2,1)S(1)} %bitcast.12, ...), custom_call_target="tpu_custom_call" | custom-call | flops 1000000000 | bytes 500000 | tf_op jit(solution)/shard_map/pallas_call | solution.py:442
  6.1 0.1 collective-permute-start
  6.2 1.6 %collective-permute-start.2 = (bf16[416,128]{1,0:T(8,128)(2,1)S(1)}, bf16[416,128]{1,0:T(8,128)(2,1)S(1)}, u32[]{:S(2)}, u32[]{:S(2)}) collective-permute-start(bf16[416,128]{1,0:T(8,128)(2,1)S(1)} %get-tuple-element.27.refs_0_), channel_id=1, source_target_pairs={{0,2},{1,3},{2,0},{3,1},{4,6},{5,7},{6,4},{7,5},{8,10},{9,11},{10,... | collective-permute-start | bytes 319496 | tf_op jit(solution)/shard_map/ppermute | solution.py:412
  7.8 2.6 %collective-permute-start.3 = (bf16[416,128]{1,0:T(8,128)(2,1)S(1)}, bf16[416,128]{1,0:T(8,128)(2,1)S(1)}, u32[]{:S(2)}, u32[]{:S(2)}) collective-permute-start(bf16[416,128]{1,0:T(8,128)(2,1)S(1)} %get-tuple-element.27.refs_0_), channel_id=1, source_target_pairs={{0,4},{1,5},{2,6},{3,7},{4,0},{5,1},{6,2},{7,3},{8,12},{9,13},{10,... | collective-permute-start | bytes 319496 | tf_op jit(solution)/shard_map/ppermute | solution.py:412
  10.4 0.0 collective-permute-done.1.message_ref
  10.4 0.8 %shard_map.115 = (f32[8,128]{1,0:T(8,128)S(1)}, bf16[2,160,160]{2,1,0:T(8,128)(2,1)S(1)}, bf16[2,160,160]{2,1,0:T(8,128)(2,1)S(1)}) custom-call(bf16[400,128]{1,0:T(8,128)(2,1)S(1)} %collective-permute-done.1.message_ref, f32[2,160,160]{2,1,0:T(8,128)S(1)} %get-tuple-element.28.im_re_ref, f32[2,160,160]{2,1,0:T(8,128)S(1)} %get-tuple-element.29.im_im_ref, ...), custom_call_target="tpu_custom_call" | custom-call | flops 1000000000 | bytes 500000 | tf_op jit(solution)/shard_map/pallas_call | solution.py:448
  11.2 1.5 %collective-permute-start.8 = (f32[8,128]{1,0:T(8,128)S(1)}, f32[8,128]{1,0:T(8,128)S(1)}, u32[]{:S(2)}, u32[]{:S(2)}) collective-permute-start(f32[8,128]{1,0:T(8,128)S(1)} %get-tuple-element.34.refs_2_.refs_0_), channel_id=1, source_target_pairs={{0,8},{8,16},{16,24},{24,0},{1,9},{9,17},{17,25},{25,1},{2,10},{10... | collective-permute-start | bytes 12296 | tf_op jit(solution)/shard_map/ppermute | solution.py:408
  12.8 0.5 %collective-permute-start.9 = (f32[8,128]{1,0:T(8,128)S(1)}, f32[8,128]{1,0:T(8,128)S(1)}, u32[]{:S(2)}, u32[]{:S(2)}) collective-permute-start(f32[8,128]{1,0:T(8,128)S(1)} %get-tuple-element.34.refs_2_.refs_0_), channel_id=1, source_target_pairs={{0,16},{8,24},{16,0},{24,8},{1,17},{9,25},{17,1},{25,9},{2,18},{10... | collective-permute-start | bytes 12296 | tf_op jit(solution)/shard_map/ppermute | solution.py:408
  13.3 0.8 %shard_map.117 = (f32[2,160,160]{2,1,0:T(8,128)S(1)}, f32[2,160,160]{2,1,0:T(8,128)S(1)}, f32[2,160,160]{2,1,0:T(8,128)S(1)}) custom-call(bf16[2,160,160]{2,1,0:T(8,128)(2,1)S(1)} %get-tuple-element.39.cross_re_ref, bf16[2,160,160]{2,1,0:T(8,128)(2,1)S(1)} %get-tuple-element.40.cross_im_ref, bf16[160,160]{1,0:T(8,128)(2,1)S(1)} %copy-done.4, ...), custom_call_target="tpu_custom_call" | custom-call | flops 1000000000 | bytes 500000 | tf_op jit(solution)/shard_map/pallas_call | solution.py:454
  14.1 0.0 collective-permute-done.refs_1_
  14.1 0.4 %shard_map.116 = (bf16[320,640]{1,0:T(8,128)(2,1)S(1)}, bf16[640,256]{1,0:T(8,128)(2,1)S(1)}, bf16[640,256]{1,0:T(8,128)(2,1)S(1)}, bf16[640,256]{1,0:T(8,128)(2,1)S(1)}) custom-call(bf16[416,128]{1,0:T(8,128)(2,1)S(1)} %get-tuple-element.27.refs_0_, bf16[416,128]{1,0:T(8,128)(2,1)S(1)} %collective-permute-done.refs_1_, ...), custom_call_target="tpu_custom_call" | custom-call | flops 1000000000 | bytes 500000 | tf_op jit(solution)/shard_map/pallas_call | solution.py:476
  14.5 1.5 %collective-permute-done.3.refs_1_ = bf16[416,128]{1,0:T(8,128)(2,1)S(1)} collective-permute-done((bf16[416,128]{1,0:T(8,128)(2,1)S(1)}, bf16[416,128]{1,0:T(8,128)(2,1)S(1)}, u32[]{:S(2)}, u32[]{:S(2)}) %collective-permute-start.3) | collective-permute-done | bytes 106528 | tf_op jit(solution)/shard_map/ppermute | solution.py:412
  16.1 0.4 %collective-permute-start.4 = (bf16[416,128]{1,0:T(8,128)(2,1)S(1)}, bf16[416,128]{1,0:T(8,128)(2,1)S(1)}, u32[]{:S(2)}, u32[]{:S(2)}) collective-permute-start(bf16[416,128]{1,0:T(8,128)(2,1)S(1)} %collective-permute-done.3.refs_1_), channel_id=1, source_target_pairs={{0,2},{1,3},{2,0},{3,1},{4,6},{5,7},{6,4},{7,5},{8,10},{9,11},{10,... | collective-permute-start | bytes 319496 | tf_op jit(solution)/shard_map/ppermute | solution.py:412
  16.5 0.0 collective-permute-done.8.refs_1_
  16.5 0.0 collective-permute-done.9.refs_2_
  16.5 0.6 %shard_map.118 = (f32[8,128]{1,0:T(8,128)S(1)}, f32[8,128]{1,0:T(8,128)S(1)}) custom-call(f32[8,128]{1,0:T(8,128)S(1)} %get-tuple-element.34.refs_2_.refs_0_, f32[8,128]{1,0:T(8,128)S(1)} %collective-permute-done.8.refs_1_, f32[8,128]{1,0:T(8,128)S(1)} %collective-permute-done.9.refs_2_, f32[2,160,160]{2,1,0:T(8,128)S(1)} %get-tuple-element.41.refs_3_.corr_ref, ...), custom_call_target="tpu_custom_call" | custom-call | flops 1000000000 | bytes 500000 | tf_op jit(solution)/shard_map/pallas_call | solution.py:488
  17.1 2.1 %collective-permute-start.12 = (f32[8,128]{1,0:T(8,128)S(1)}, f32[8,128]{1,0:T(8,128)S(1)}, u32[]{:S(2)}, u32[]{:S(2)}) collective-permute-start(f32[8,128]{1,0:T(8,128)S(1)} %get-tuple-element.45.smooth_ref), channel_id=1, source_target_pairs={{0,6},{1,7},{2,4},{3,5},{4,2},{5,3},{6,0},{7,1},{8,14},{9,15},{10,... | collective-permute-start | bytes 12296 | tf_op jit(solution)/shard_map/ppermute | solution.py:412
  19.2 1.0 %collective-permute-start.11 = (f32[8,128]{1,0:T(8,128)S(1)}, f32[8,128]{1,0:T(8,128)S(1)}, u32[]{:S(2)}, u32[]{:S(2)}) collective-permute-start(f32[8,128]{1,0:T(8,128)S(1)} %get-tuple-element.45.smooth_ref), channel_id=1, source_target_pairs={{0,4},{1,5},{2,6},{3,7},{4,0},{5,1},{6,2},{7,3},{8,12},{9,13},{10,... | collective-permute-start | bytes 12296 | tf_op jit(solution)/shard_map/ppermute | solution.py:412
  20.2 1.3 %collective-permute-start.10 = (f32[8,128]{1,0:T(8,128)S(1)}, f32[8,128]{1,0:T(8,128)S(1)}, u32[]{:S(2)}, u32[]{:S(2)}) collective-permute-start(f32[8,128]{1,0:T(8,128)S(1)} %get-tuple-element.45.smooth_ref), channel_id=1, source_target_pairs={{0,2},{1,3},{2,0},{3,1},{4,6},{5,7},{6,4},{7,5},{8,10},{9,11},{10,... | collective-permute-start | bytes 12296 | tf_op jit(solution)/shard_map/ppermute | solution.py:412
  21.6 0.9 %shard_map.119 = (f32[2,160,160]{2,1,0:T(8,128)}, f32[8,128]{1,0:T(8,128)S(1)}) custom-call(f32[2,160,160]{2,1,0:T(8,128)S(1)} %get-tuple-element.41.refs_3_.corr_ref, f32[2,160,160]{2,1,0:T(8,128)S(1)} %get-tuple-element.42.grad_y_ref, f32[2,160,160]{2,1,0:T(8,128)S(1)} %get-tuple-element.43.grad_x_ref, f32[8,128]{1,0:T(8,128)S(1)} %get-tuple-element.44.prior_ref, ...), custom_call_target="tpu_custom_call" | custom-call | flops 1000000000 | bytes 500000 | tf_op jit(solution)/shard_map/pallas_call | solution.py:493
  22.4 0.0 collective-permute-done.2.refs_0_
  22.4 0.0 collective-permute-start.6
  22.4 0.1 collective-permute-done.12
  22.6 0.4 %collective-permute-start.5 = (bf16[416,128]{1,0:T(8,128)(2,1)S(1)}, bf16[416,128]{1,0:T(8,128)(2,1)S(1)}, u32[]{:S(2)}, u32[]{:S(2)}) collective-permute-start(bf16[416,128]{1,0:T(8,128)(2,1)S(1)} %collective-permute-done.2.refs_0_), channel_id=1, source_target_pairs={{0,1},{1,0},{2,3},{3,2},{4,5},{5,4},{6,7},{7,6},{8,9},{9,8},{10,11... | collective-permute-start | bytes 319496 | tf_op jit(solution)/shard_map/ppermute | solution.py:412
  22.9 0.0 collective-permute-done.4.refs_2_
  22.9 0.1 collective-permute-start.7
  23.1 0.6 %collective-permute-done.11 = f32[8,128]{1,0:T(8,128)S(1)} collective-permute-done((f32[8,128]{1,0:T(8,128)S(1)}, f32[8,128]{1,0:T(8,128)S(1)}, u32[]{:S(2)}, u32[]{:S(2)}) %collective-permute-start.11) | collective-permute-done | bytes 4128 | tf_op jit(solution)/shard_map/ppermute | solution.py:412
  23.7 0.1 collective-permute-done.10
  23.8 0.0 collective-permute-start.13
  23.8 0.1 collective-permute-done.5.refs_3_
  23.9 0.0 collective-permute-done.6.refs_4_
  23.9 0.4 %collective-permute-done.7.refs_5_ = bf16[416,128]{1,0:T(8,128)(2,1)S(1)} collective-permute-done((bf16[416,128]{1,0:T(8,128)(2,1)S(1)}, bf16[416,128]{1,0:T(8,128)(2,1)S(1)}, u32[]{:S(2)}, u32[]{:S(2)}) %collective-permute-start.7) | collective-permute-done | bytes 106528 | tf_op jit(solution)/shard_map/ppermute | solution.py:412
  24.3 1.0 %shard_map.120 = (bf16[320,1920]{1,0:T(8,128)(2,1)S(1)}, bf16[1920,256]{1,0:T(8,128)(2,1)S(1)}, bf16[1920,256]{1,0:T(8,128)(2,1)S(1)}, bf16[1920,256]{1,0:T(8,128)(2,1)S(1)}) custom-call(bf16[416,128]{1,0:T(8,128)(2,1)S(1)} %collective-permute-done.2.refs_0_, bf16[416,128]{1,0:T(8,128)(2,1)S(1)} %collective-permute-done.3.refs_1_, ...), custom_call_target="tpu_custom_call" | custom-call | flops 1000000000 | bytes 500000 | tf_op jit(solution)/shard_map/pallas_call | solution.py:476
  25.2 0.0 collective-permute-done.13.refs_9_
  25.2 1.6 %shard_map.121 = bf16[160,320]{1,0:T(8,128)(2,1)} custom-call(bf16[320,640]{1,0:T(8,128)(2,1)S(1)} %get-tuple-element.35.refs_4_.refs_0_, bf16[640,256]{1,0:T(8,128)(2,1)S(1)} %get-tuple-element.36.refs_1_, bf16[640,256]{1,0:T(8,128)(2,1)S(1)} %get-tuple-element.37.refs_2_, bf16[640,256]{1,0:T(8,128)(2,1)S(1)} %get-tuple-element.38.refs_3_, ...), custom_call_target="tpu_custom_call" | custom-call | flops 1000000000 | bytes 500000 | tf_op jit(solution)/shard_map/pallas_call | solution.py:502
  (1 shorter events, 0.0 us)
Async XLA Ops:
  0.6 4.7 %copy-start = (bf16[1,2,160,160]{3,2,1,0:T(8,128)(2,1)S(1)}, bf16[1,2,160,160]{3,2,1,0:T(8,128)(2,1)}, u32[]{:S(2)}) copy-start(bf16[1,2,160,160]{3,2,1,0:T(8,128)(2,1)} %param.10) | copy-start | bytes 307204
  0.6 4.7 %copy-start.1 = (s32[1,320,1]{1,2,0:T(1,128)S(1)}, s32[1,320,1]{1,2,0:T(1,128)}, u32[]{:S(2)}) copy-start(s32[1,320,1]{1,2,0:T(1,128)} %param.16) | copy-start | bytes 3844
  0.7 4.7 %copy-start.2 = (s32[1,320]{1,0:T(1,128)S(1)}, s32[1,320]{1,0:T(1,128)}, u32[]{:S(2)}) copy-start(s32[1,320]{1,0:T(1,128)} %target_ref.1) | copy-start | bytes 3844
  0.7 4.7 %copy-start.3 = (s32[1,2,2]{2,1,0:T(2,128)S(1)}, s32[1,2,2]{2,1,0:T(2,128)}, u32[]{:S(2)}) copy-start(s32[1,2,2]{2,1,0:T(2,128)} %param.11) | copy-start | bytes 52
  0.7 4.7 %copy-start.4 = (bf16[160,160]{1,0:T(8,128)(2,1)S(1)}, bf16[160,160]{1,0:T(8,128)(2,1)}, u32[]{:S(2)}) copy-start(bf16[160,160]{1,0:T(8,128)(2,1)} %constant.4.clone.cos_ref) | copy-start | bytes 153604
  0.7 4.7 %copy-start.5 = (bf16[160,160]{1,0:T(8,128)(2,1)S(1)}, bf16[160,160]{1,0:T(8,128)(2,1)}, u32[]{:S(2)}) copy-start(bf16[160,160]{1,0:T(8,128)(2,1)} %constant.5.clone.sin_ref) | copy-start | bytes 153604
  2.3 8.1 %collective-permute-start.1 = (bf16[400,128]{1,0:T(8,128)(2,1)S(1)}, bf16[400,128]{1,0:T(8,128)(2,1)S(1)}, u32[]{:S(2)}, u32[]{:S(2)}) collective-permute-start(bf16[400,128]{1,0:T(8,128)(2,1)S(1)} %shard_map.113.base_ref), channel_id=1, source_target_pairs={{0,8},{8,16},{16,24},{24,0},{1,9},{9,17},{17,25},{25,1},{2,10},{10... | collective-permute-start | bytes 307208 | tf_op jit(solution)/shard_map/ppermute | solution.py:408
  6.1 8.0 %collective-permute-start = (bf16[416,128]{1,0:T(8,128)(2,1)S(1)}, bf16[416,128]{1,0:T(8,128)(2,1)S(1)}, u32[]{:S(2)}, u32[]{:S(2)}) collective-permute-start(bf16[416,128]{1,0:T(8,128)(2,1)S(1)} %get-tuple-element.27.refs_0_), channel_id=1, source_target_pairs={{0,1},{1,0},{2,3},{3,2},{4,5},{5,4},{6,7},{7,6},{8,9},{9,8},{10,11... | collective-permute-start | bytes 319496 | tf_op jit(solution)/shard_map/ppermute | solution.py:412
  6.2 16.2 %collective-permute-start.2 = (bf16[416,128]{1,0:T(8,128)(2,1)S(1)}, bf16[416,128]{1,0:T(8,128)(2,1)S(1)}, u32[]{:S(2)}, u32[]{:S(2)}) collective-permute-start(bf16[416,128]{1,0:T(8,128)(2,1)S(1)} %get-tuple-element.27.refs_0_), channel_id=1, source_target_pairs={{0,2},{1,3},{2,0},{3,1},{4,6},{5,7},{6,4},{7,5},{8,10},{9,11},{10,... | collective-permute-start | bytes 319496 | tf_op jit(solution)/shard_map/ppermute | solution.py:412
  7.8 8.3 %collective-permute-start.3 = (bf16[416,128]{1,0:T(8,128)(2,1)S(1)}, bf16[416,128]{1,0:T(8,128)(2,1)S(1)}, u32[]{:S(2)}, u32[]{:S(2)}) collective-permute-start(bf16[416,128]{1,0:T(8,128)(2,1)S(1)} %get-tuple-element.27.refs_0_), channel_id=1, source_target_pairs={{0,4},{1,5},{2,6},{3,7},{4,0},{5,1},{6,2},{7,3},{8,12},{9,13},{10,... | collective-permute-start | bytes 319496 | tf_op jit(solution)/shard_map/ppermute | solution.py:412
  11.2 5.3 %collective-permute-start.8 = (f32[8,128]{1,0:T(8,128)S(1)}, f32[8,128]{1,0:T(8,128)S(1)}, u32[]{:S(2)}, u32[]{:S(2)}) collective-permute-start(f32[8,128]{1,0:T(8,128)S(1)} %get-tuple-element.34.refs_2_.refs_0_), channel_id=1, source_target_pairs={{0,8},{8,16},{16,24},{24,0},{1,9},{9,17},{17,25},{25,1},{2,10},{10... | collective-permute-start | bytes 12296 | tf_op jit(solution)/shard_map/ppermute | solution.py:408
  12.8 3.8 %collective-permute-start.9 = (f32[8,128]{1,0:T(8,128)S(1)}, f32[8,128]{1,0:T(8,128)S(1)}, u32[]{:S(2)}, u32[]{:S(2)}) collective-permute-start(f32[8,128]{1,0:T(8,128)S(1)} %get-tuple-element.34.refs_2_.refs_0_), channel_id=1, source_target_pairs={{0,16},{8,24},{16,0},{24,8},{1,17},{9,25},{17,1},{25,9},{2,18},{10... | collective-permute-start | bytes 12296 | tf_op jit(solution)/shard_map/ppermute | solution.py:408
  16.1 6.9 %collective-permute-start.4 = (bf16[416,128]{1,0:T(8,128)(2,1)S(1)}, bf16[416,128]{1,0:T(8,128)(2,1)S(1)}, u32[]{:S(2)}, u32[]{:S(2)}) collective-permute-start(bf16[416,128]{1,0:T(8,128)(2,1)S(1)} %collective-permute-done.3.refs_1_), channel_id=1, source_target_pairs={{0,2},{1,3},{2,0},{3,1},{4,6},{5,7},{6,4},{7,5},{8,10},{9,11},{10,... | collective-permute-start | bytes 319496 | tf_op jit(solution)/shard_map/ppermute | solution.py:412
  17.1 5.5 %collective-permute-start.12 = (f32[8,128]{1,0:T(8,128)S(1)}, f32[8,128]{1,0:T(8,128)S(1)}, u32[]{:S(2)}, u32[]{:S(2)}) collective-permute-start(f32[8,128]{1,0:T(8,128)S(1)} %get-tuple-element.45.smooth_ref), channel_id=1, source_target_pairs={{0,6},{1,7},{2,4},{3,5},{4,2},{5,3},{6,0},{7,1},{8,14},{9,15},{10,... | collective-permute-start | bytes 12296 | tf_op jit(solution)/shard_map/ppermute | solution.py:412
  19.2 4.5 %collective-permute-start.11 = (f32[8,128]{1,0:T(8,128)S(1)}, f32[8,128]{1,0:T(8,128)S(1)}, u32[]{:S(2)}, u32[]{:S(2)}) collective-permute-start(f32[8,128]{1,0:T(8,128)S(1)} %get-tuple-element.45.smooth_ref), channel_id=1, source_target_pairs={{0,4},{1,5},{2,6},{3,7},{4,0},{5,1},{6,2},{7,3},{8,12},{9,13},{10,... | collective-permute-start | bytes 12296 | tf_op jit(solution)/shard_map/ppermute | solution.py:412
  20.2 3.6 %collective-permute-start.10 = (f32[8,128]{1,0:T(8,128)S(1)}, f32[8,128]{1,0:T(8,128)S(1)}, u32[]{:S(2)}, u32[]{:S(2)}) collective-permute-start(f32[8,128]{1,0:T(8,128)S(1)} %get-tuple-element.45.smooth_ref), channel_id=1, source_target_pairs={{0,2},{1,3},{2,0},{3,1},{4,6},{5,7},{6,4},{7,5},{8,10},{9,11},{10,... | collective-permute-start | bytes 12296 | tf_op jit(solution)/shard_map/ppermute | solution.py:412
  22.4 1.5 %collective-permute-start.6 = (bf16[416,128]{1,0:T(8,128)(2,1)S(1)}, bf16[416,128]{1,0:T(8,128)(2,1)S(1)}, u32[]{:S(2)}, u32[]{:S(2)}) collective-permute-start(bf16[416,128]{1,0:T(8,128)(2,1)S(1)} %collective-permute-done.3.refs_1_), channel_id=1, source_target_pairs={{0,1},{1,0},{2,3},{3,2},{4,5},{5,4},{6,7},{7,6},{8,9},{9,8},{10,11... | collective-permute-start | bytes 319496 | tf_op jit(solution)/shard_map/ppermute | solution.py:412
  22.6 1.3 %collective-permute-start.5 = (bf16[416,128]{1,0:T(8,128)(2,1)S(1)}, bf16[416,128]{1,0:T(8,128)(2,1)S(1)}, u32[]{:S(2)}, u32[]{:S(2)}) collective-permute-start(bf16[416,128]{1,0:T(8,128)(2,1)S(1)} %collective-permute-done.2.refs_0_), channel_id=1, source_target_pairs={{0,1},{1,0},{2,3},{3,2},{4,5},{5,4},{6,7},{7,6},{8,9},{9,8},{10,11... | collective-permute-start | bytes 319496 | tf_op jit(solution)/shard_map/ppermute | solution.py:412
  22.9 1.3 %collective-permute-start.7 = (bf16[416,128]{1,0:T(8,128)(2,1)S(1)}, bf16[416,128]{1,0:T(8,128)(2,1)S(1)}, u32[]{:S(2)}, u32[]{:S(2)}) collective-permute-start(bf16[416,128]{1,0:T(8,128)(2,1)S(1)} %collective-permute-done.4.refs_2_), channel_id=1, source_target_pairs={{0,1},{1,0},{2,3},{3,2},{4,5},{5,4},{6,7},{7,6},{8,9},{9,8},{10,11... | collective-permute-start | bytes 319496 | tf_op jit(solution)/shard_map/ppermute | solution.py:412
  23.8 1.4 %collective-permute-start.13 = (f32[8,128]{1,0:T(8,128)S(1)}, f32[8,128]{1,0:T(8,128)S(1)}, u32[]{:S(2)}, u32[]{:S(2)}) collective-permute-start(f32[8,128]{1,0:T(8,128)S(1)} %add_add_fusion.refs_6_.refs_8_), channel_id=1, source_target_pairs={{0,1},{1,0},{2,3},{3,2},{4,5},{5,4},{6,7},{7,6},{8,9},{9,8},{10,11... | collective-permute-start | bytes 12296 | tf_op jit(solution)/shard_map/ppermute | solution.py:412
